TPU v7x, 512 devices: a whole 4x8x8 slice. The times are simulated.
512 devices in a mesh: stream: 8 (over x, core), span: 8 (over z), depth: 8 (over y).
Axes of the slice: x: 4, y: 8, z: 8, core: 2. Of those that a mesh axis runs over, the one named last changes fastest.
Arguments:
- old_adjoint: float32 [3, 4096, 4096], P(None, ('stream', 'span', 'depth')), may hold values from -6 to 6
- target: int32 [4096], P(('stream', 'span', 'depth')), may hold values from 0 to 511, as said below
- velocity: bfloat16 [3, 128, 128, 1024], P(None, 'stream', 'span', 'depth'), may hold values from -3 to 3
- chi: float32 [128, 128, 1024], P('stream', 'span', 'depth'), may hold values from 0 to 1
- fish: int32 [8, 8, 64], P('stream', 'span', 'depth'), may hold values from 0 to 63
- fish_forcing: float32 [64, 3], replicated, may hold values from -6 to 6
Outputs:
- adjoint: float32 [3, 128, 128, 1024], P(None, 'stream', 'span', 'depth')
Inputs may be any that keep to these rules, and one draw needn't show every extreme that they name: `target`: within each depth index, the 64 devices' entries name every number from 0 to 511 once. Each device sends its blocks to exactly 8 devices of its depth index, 1 block to each, and each device receives 1 block from each of 8 devices.
All inputs are finite; a program needn't handle non-finite values.
Results may differ from a plain program's by a relative error of at most 0.0003.
Values may be sent and summed in bfloat16 or wider, within the bound.
A program may use at most 64 MiB of HBM per device.

v0:
```python
import jax
import jax.numpy as jnp
from jax import lax
from jax.sharding import PartitionSpec as P

SECTIONS = 2


advect_coef = 0.1
diffuse_coef = 0.1


def extended(cells, sides, width):
    for axis, dim in sides:
        count = lax.axis_size(axis)
        ends = count - 1
        head = lax.slice_in_dim(cells, 0, width, axis=dim)
        tail = lax.slice_in_dim(cells, cells.shape[dim] - width, cells.shape[dim], axis=dim)
        cells = jnp.concatenate(
            [
                lax.ppermute(tail, axis, [(i, (i + 1) % count) for i in range(ends)]),
                cells,
                lax.ppermute(head, axis, [((i + 1) % count, i) for i in range(ends)]),
            ],
            axis=dim,
        )
    return cells


def interior(field):
    return field[:, 1:-1, 1:-1, 1:-1]


def offset(field, axis_num, shift_by):
    selection = [slice(None), slice(1, -1), slice(1, -1), slice(1, -1)]
    selection[axis_num] = slice(1 + shift_by, field.shape[axis_num] - 1 + shift_by)
    return field[tuple(selection)]


def centered(field, axis_num):
    return offset(field, axis_num, 1) - offset(field, axis_num, -1)


def advect(padded, carried, slopes):
    current = interior(padded)
    transport = (
        carried[0:1] * centered(padded, 1)
        + carried[1:2] * centered(padded, 2)
        + carried[2:3] * centered(padded, 3)
    )
    stretching = jnp.stack([jnp.sum(current * slopes[axis_num], axis=0) for axis_num in range(3)])
    return current + advect_coef * (transport - stretching)


def diffuse(padded):
    centre = interior(padded)
    total = offset(padded, 1, 1) + offset(padded, 1, -1)
    total = total + offset(padded, 2, 1) + offset(padded, 2, -1)
    total = total + offset(padded, 3, 1) + offset(padded, 3, -1)
    return centre + diffuse_coef * (total - 6.0 * centre)


def body(old_adjoint, target, velocity, chi, fish, fish_forcing):
    block_count = target.shape[0]
    members = lax.axis_size(("stream", "span"))
    capacity = max(1, block_count // members)
    block_cells = old_adjoint.shape[2]
    indices = jnp.arange(block_count)
    owner_rank = target // block_count
    new_slot = target % block_count
    earlier = (owner_rank[None, :] == owner_rank[:, None]) & (indices[None, :] < indices[:, None])
    send_rank = jnp.sum(earlier.astype(jnp.int32), axis=1)
    buffer_pos = owner_rank * capacity + send_rank
    outgoing = (
        jnp.zeros((3, members * capacity, block_cells), jnp.float32)
        .at[:, buffer_pos]
        .set(old_adjoint)
    )
    labels = (
        jnp.full((1, members * capacity), float(block_count), jnp.float32)
        .at[0, buffer_pos]
        .set(new_slot.astype(jnp.float32))
    )
    incoming, moved_labels = (
        lax.all_to_all(outgoing, ("stream", "span"), split_axis=1, concat_axis=1, tiled=True),
        lax.all_to_all(labels, ("stream", "span"), split_axis=1, concat_axis=1, tiled=True),
    )
    incoming_labels = moved_labels[0]
    placed = (
        jnp.zeros((3, block_count, block_cells), jnp.float32)
        .at[:, incoming_labels.astype(jnp.int32)]
        .set(incoming, mode="drop")
    )
    blocks_x, blocks_y, blocks_z = fish.shape
    block_edge = velocity.shape[1] // blocks_x
    adjoint = placed.reshape(3, blocks_x, blocks_y, blocks_z, block_edge, block_edge, block_edge)
    adjoint = adjoint.transpose(0, 1, 4, 2, 5, 3, 6).reshape(velocity.shape)
    rim_width = 2
    wide_velocity = extended(
        velocity, (("stream", 1), ("span", 2), ("depth", 3)), rim_width
    ).astype(jnp.float32)
    carried = interior(wide_velocity)
    slopes = [centered(wide_velocity, axis_num) for axis_num in (1, 2, 3)]
    fish_ids = fish.reshape(-1)
    onehot = (jnp.arange(fish_forcing.shape[0])[:, None] == fish_ids[None, :]).astype(jnp.float32)
    per_block = jnp.dot(fish_forcing.T, onehot, precision=lax.Precision.HIGHEST).reshape(
        3, blocks_x, blocks_y, blocks_z
    )
    forcing = jnp.broadcast_to(
        per_block[:, :, None, :, None, :, None],
        (3, blocks_x, block_edge, blocks_y, block_edge, blocks_z, block_edge),
    ).reshape(velocity.shape)
    chi_wide = chi[None]
    for section_num in range(SECTIONS):
        padded = extended(adjoint, (("stream", 1), ("span", 2), ("depth", 3)), 1)
        advected = advect(padded, interior(carried), [interior(slope_now) for slope_now in slopes])
        mixed_field = diffuse(extended(advected, (("stream", 1), ("span", 2), ("depth", 3)), 1))
        adjoint = (mixed_field + chi_wide * forcing) / (1.0 + chi_wide)
    return adjoint


def solution(mesh):
    return jax.shard_map(
        body,
        mesh=mesh,
        in_specs=(
            P(None, ("stream", "span", "depth"), None),
            P(("stream", "span", "depth")),
            P(None, "stream", "span", "depth"),
            P("stream", "span", "depth"),
            P("stream", "span", "depth"),
            P(),
        ),
        out_specs=P(None, "stream", "span", "depth"),
        check_vma=False,
    )
```

profile of v0, /device:TPU:1, one launch (start us, length us, event | category | flops | bytes accessed | tf_op | source)
XLA Modules:
  0.0 284.0 jit_solution(6117297790616002655)
XLA Ops:
  2.2 14.8 %all-to-all-start = ((f32[1,64,1]{2,0,1:T(1,128)}), f32[1,64,1]{2,0,1:T(1,128)S(1)}, u32[]{:S(2)}, u32[]{:S(2)}) async-start(f32[1,64,1]{2,0,1:T(1,128)} %copy.54), calls=%async_computation | async-start | bytes 65536 | tf_op jit(solution)/shard_map/all_to_all | solution.py:86
  18.3 3.1 %broadcast_in_dim.32 = f32[3,64,4096]{2,0,1:T(4,128)} broadcast(f32[]{:T(128)} %constant.18.clone.1), dimensions={} | broadcast | bytes 3145732 | tf_op jit(solution)/shard_map/broadcast_in_dim | solution.py:75
  26.2 8.3 %all-to-all-start.1 = ((f32[3,64,4096]{2,0,1:T(4,128)}), f32[3,64,4096]{2,0,1:T(4,128)}, u32[]{:S(2)}, u32[]{:S(2)}) async-start(f32[3,64,4096]{2,0,1:T(4,128)} %scatter_fusion), calls=%async_computation.1 | async-start | bytes 8388608 | tf_op jit(solution)/shard_map/all_to_all | solution.py:85
  34.5 3.5 %collective-permute-start = (bf16[3,2,16,128]{3,2,1,0:T(8,128)(2,1)S(1)}, bf16[3,2,16,128]{3,2,1,0:T(8,128)(2,1)S(1)}, u32[]{:S(2)}, u32[]{:S(2)}) collective-permute-start(bf16[3,2,16,128]{3,2,1,0:T(8,128)(2,1)S(1)} %get-tuple-element.51), channel_id=1, source_target_pairs={{0,64},{64,128},{128,192},{192,256},{256,320},{320,384},{384,448},... | collective-permute-start | bytes 73736 | tf_op jit(solution)/shard_map/ppermute | solution.py:21
  41.8 5.5 %collective-permute-done.1 = bf16[3,2,16,128]{3,2,1,0:T(8,128)(2,1)S(1)} collective-permute-done((bf16[3,2,16,128]{3,2,1,0:T(8,128)(2,1)S(1)}, bf16[3,2,16,128]{3,2,1,0:T(8,128)(2,1)S(1)}, u32[]{:S(2)}, u32[]{:S(2)}) %collective-permute-start.1) | collective-permute-done | bytes 24608 | tf_op jit(solution)/shard_map/ppermute | solution.py:23
  51.4 70.9 %collective-permute-done.2 = bf16[3,20,2,128]{3,2,1,0:T(2,128)(2,1)S(1)} collective-permute-done((bf16[3,20,2,128]{3,2,1,0:T(2,128)(2,1)S(1)}, bf16[3,20,2,128]{3,2,1,0:T(2,128)(2,1)S(1)}, u32[]{:S(2)}, u32[]{:S(2)}) %collective-permute-start.2) | collective-permute-done | bytes 30752 | tf_op jit(solution)/shard_map/ppermute | solution.py:21
  122.3 4.3 %collective-permute-done.3 = bf16[3,20,2,128]{3,2,1,0:T(2,128)(2,1)S(1)} collective-permute-done((bf16[3,20,2,128]{3,2,1,0:T(2,128)(2,1)S(1)}, bf16[3,20,2,128]{3,2,1,0:T(2,128)(2,1)S(1)}, u32[]{:S(2)}, u32[]{:S(2)}) %collective-permute-start.3) | collective-permute-done | bytes 30752 | tf_op jit(solution)/shard_map/ppermute | solution.py:23
  126.9 3.2 %collective-permute-start.4 = (bf16[3,20,20,2]{3,2,1,0:T(8,128)(2,1)S(1)}, bf16[3,20,20,2]{3,2,1,0:T(8,128)(2,1)S(1)}, u32[]{:S(2)}, u32[]{:S(2)}) collective-permute-start(bf16[3,20,20,2]{3,2,1,0:T(8,128)(2,1)S(1)} %get-tuple-element.46), channel_id=1, source_target_pairs={{0,1},{1,2},{2,3},{3,4},{4,5},{5,6},{6,7},{8,9},{9,10},{10,11},{11... | collective-permute-start | bytes 14408 | tf_op jit(solution)/shard_map/ppermute | solution.py:21
  131.5 5.4 %collective-permute-done.4 = bf16[3,20,20,2]{3,2,1,0:T(8,128)(2,1)S(1)} collective-permute-done((bf16[3,20,20,2]{3,2,1,0:T(8,128)(2,1)S(1)}, bf16[3,20,20,2]{3,2,1,0:T(8,128)(2,1)S(1)}, u32[]{:S(2)}, u32[]{:S(2)}) %collective-permute-start.4) | collective-permute-done | bytes 4832 | tf_op jit(solution)/shard_map/ppermute | solution.py:21
  136.9 3.9 %collective-permute-done.5 = bf16[3,20,20,2]{3,2,1,0:T(8,128)(2,1)S(1)} collective-permute-done((bf16[3,20,20,2]{3,2,1,0:T(8,128)(2,1)S(1)}, bf16[3,20,20,2]{3,2,1,0:T(8,128)(2,1)S(1)}, u32[]{:S(2)}, u32[]{:S(2)}) %collective-permute-start.5) | collective-permute-done | bytes 4832 | tf_op jit(solution)/shard_map/ppermute | solution.py:23
  142.3 7.4 %scatter_fusion.1 = f32[3,8,4096]{2,0,1:T(4,128)S(1)} fusion(f32[3,8,4096]{2,0,1:T(4,128)S(1)} %broadcast_in_dim.14, s32[64]{0:T(128)S(1)} %fusion.43, f32[64,3,4096]{2,1,0:T(4,128)} %bitcast.3), kind=kCustom, calls=%fused_computation.2 | custom fusion | bytes 9437440 | tf_op jit(solution)/shard_map/scatter | solution.py:92
  152.7 5.4 %copy.57 = f32[3,1,16,1,16,8,16]{6,5,4,2,0,3,1:T(8,128)} copy(f32[3,1,16,1,16,8,16]{6,4,2,5,0,3,1:T(8,128)} %bitcast.31) | data formatting | bytes 786432 | tf_op jit(solution)/shard_map/transpose | solution.py:97
  160.5 5.5 %collective-permute-start.7 = (f32[3,1,16,128]{3,2,1,0:T(8,128)S(1)}, f32[3,1,16,128]{3,2,1,0:T(8,128)S(1)}, u32[]{:S(2)}, u32[]{:S(2)}) collective-permute-start(f32[3,1,16,128]{3,2,1,0:T(8,128)S(1)} %get-tuple-element.45), channel_id=1, source_target_pairs={{0,64},{64,128},{128,192},{192,256},{256,320},{320,384},{384,448},... | collective-permute-start | bytes 73736 | tf_op jit(solution)/shard_map/ppermute | solution.py:21
  176.6 3.7 %collective-permute-done.8 = f32[3,18,1,128]{3,2,1,0:T(1,128)S(1)} collective-permute-done((f32[3,18,1,128]{3,2,1,0:T(1,128)S(1)}, f32[3,18,1,128]{3,2,1,0:T(1,128)S(1)}, u32[]{:S(2)}, u32[]{:S(2)}) %collective-permute-start.8) | collective-permute-done | bytes 27680 | tf_op jit(solution)/shard_map/ppermute | solution.py:23
  182.1 3.2 %collective-permute-start.11 = (f32[3,18,18,1]{2,3,1,0:T(1,128)S(1)}, f32[3,18,18,1]{2,3,1,0:T(1,128)S(1)}, u32[]{:S(2)}, u32[]{:S(2)}) collective-permute-start(f32[3,18,18,1]{2,3,1,0:T(1,128)S(1)} %copy.60), channel_id=1, source_target_pairs={{0,1},{1,2},{2,3},{3,4},{4,5},{5,6},{6,7},{8,9},{9,10},{10,11},{11... | collective-permute-start | bytes 11672 | tf_op jit(solution)/shard_map/ppermute | solution.py:21
  194.3 4.4 %collective-permute-start.13 = (f32[3,1,16,128]{3,2,1,0:T(8,128)S(1)}, f32[3,1,16,128]{3,2,1,0:T(8,128)S(1)}, u32[]{:S(2)}, u32[]{:S(2)}) collective-permute-start(f32[3,1,16,128]{3,2,1,0:T(8,128)S(1)} %get-tuple-element.41), channel_id=1, source_target_pairs={{0,64},{64,128},{128,192},{192,256},{256,320},{320,384},{384,448},... | collective-permute-start | bytes 73736 | tf_op jit(solution)/shard_map/ppermute | solution.py:21
  200.6 3.2 %collective-permute-done.12 = f32[3,1,16,128]{3,2,1,0:T(8,128)S(1)} collective-permute-done((f32[3,1,16,128]{3,2,1,0:T(8,128)S(1)}, f32[3,1,16,128]{3,2,1,0:T(8,128)S(1)}, u32[]{:S(2)}, u32[]{:S(2)}) %collective-permute-start.12) | collective-permute-done | bytes 24608 | tf_op jit(solution)/shard_map/ppermute | solution.py:23
  203.9 4.5 %collective-permute-start.15 = (f32[3,18,1,128]{3,2,1,0:T(1,128)S(1)}, f32[3,18,1,128]{3,2,1,0:T(1,128)S(1)}, u32[]{:S(2)}, u32[]{:S(2)}) collective-permute-start(f32[3,18,1,128]{3,2,1,0:T(1,128)S(1)} %get-tuple-element.33), channel_id=1, source_target_pairs={{0,8},{8,16},{16,24},{24,32},{32,40},{40,48},{48,56},{1,9},{9,17},... | collective-permute-start | bytes 82952 | tf_op jit(solution)/shard_map/ppermute | solution.py:21
  210.4 2.9 %collective-permute-done.14 = f32[3,18,1,128]{3,2,1,0:T(1,128)S(1)} collective-permute-done((f32[3,18,1,128]{3,2,1,0:T(1,128)S(1)}, f32[3,18,1,128]{3,2,1,0:T(1,128)S(1)}, u32[]{:S(2)}, u32[]{:S(2)}) %collective-permute-start.14) | collective-permute-done | bytes 27680 | tf_op jit(solution)/shard_map/ppermute | solution.py:23
  214.5 4.6 %collective-permute-start.17 = (f32[3,18,18,1]{2,3,1,0:T(1,128)S(1)}, f32[3,18,18,1]{2,3,1,0:T(1,128)S(1)}, u32[]{:S(2)}, u32[]{:S(2)}) collective-permute-start(f32[3,18,18,1]{2,3,1,0:T(1,128)S(1)} %copy.64), channel_id=1, source_target_pairs={{0,1},{1,2},{2,3},{3,4},{4,5},{5,6},{6,7},{8,9},{9,10},{10,11},{11... | collective-permute-start | bytes 11672 | tf_op jit(solution)/shard_map/ppermute | solution.py:21
  220.7 3.3 %collective-permute-done.16 = f32[3,18,18,1]{2,3,1,0:T(1,128)S(1)} collective-permute-done((f32[3,18,18,1]{2,3,1,0:T(1,128)S(1)}, f32[3,18,18,1]{2,3,1,0:T(1,128)S(1)}, u32[]{:S(2)}, u32[]{:S(2)}) %collective-permute-start.16) | collective-permute-done | bytes 3920 | tf_op jit(solution)/shard_map/ppermute | solution.py:23
  224.9 4.7 %multiply_reduce_fusion.2 = (f32[16,16,128]{2,1,0:T(8,128)}, f32[16,16,128]{2,1,0:T(8,128)}, f32[16,16,128]{2,1,0:T(8,128)}, f32[3,16,16,128]{3,2,1,0:T(8,128)S(1)}) fusion(f32[3,18,18,130]{3,2,1,0:T(8,128)} %copy-done.1, f32[3,18,18,130]{3,2,1,0:T(8,128)} %copy-done.2, f32[3,18,18,130]{3,2,1,0:T(8,128)} %copy-done.5, f32[3,18,18,130]{3,2,1,0:T(8,128)} %copy-done.4, ...), kind=kLoop, calls=%fused_computation.120 | loop fusion | flops 3735552 | bytes 3914848 | tf_op jit(solution)/shard_map/reduce_sum | solution.py:51
  229.6 4.3 %collective-permute-start.19 = (f32[3,1,16,128]{3,2,1,0:T(8,128)S(1)}, f32[3,1,16,128]{3,2,1,0:T(8,128)S(1)}, u32[]{:S(2)}, u32[]{:S(2)}) collective-permute-start(f32[3,1,16,128]{3,2,1,0:T(8,128)S(1)} %get-tuple-element.39), channel_id=1, source_target_pairs={{0,64},{64,128},{128,192},{192,256},{256,320},{320,384},{384,448},... | collective-permute-start | bytes 73736 | tf_op jit(solution)/shard_map/ppermute | solution.py:21
  235.8 3.2 %collective-permute-done.18 = f32[3,1,16,128]{3,2,1,0:T(8,128)S(1)} collective-permute-done((f32[3,1,16,128]{3,2,1,0:T(8,128)S(1)}, f32[3,1,16,128]{3,2,1,0:T(8,128)S(1)}, u32[]{:S(2)}, u32[]{:S(2)}) %collective-permute-start.18) | collective-permute-done | bytes 24608 | tf_op jit(solution)/shard_map/ppermute | solution.py:23
  239.1 4.1 %collective-permute-start.21 = (f32[3,18,1,128]{3,2,1,0:T(1,128)S(1)}, f32[3,18,1,128]{3,2,1,0:T(1,128)S(1)}, u32[]{:S(2)}, u32[]{:S(2)}) collective-permute-start(f32[3,18,1,128]{3,2,1,0:T(1,128)S(1)} %get-tuple-element.31), channel_id=1, source_target_pairs={{0,8},{8,16},{16,24},{24,32},{32,40},{40,48},{48,56},{1,9},{9,17},... | collective-permute-start | bytes 82952 | tf_op jit(solution)/shard_map/ppermute | solution.py:21
  244.5 3.3 %collective-permute-done.20 = f32[3,18,1,128]{3,2,1,0:T(1,128)S(1)} collective-permute-done((f32[3,18,1,128]{3,2,1,0:T(1,128)S(1)}, f32[3,18,1,128]{3,2,1,0:T(1,128)S(1)}, u32[]{:S(2)}, u32[]{:S(2)}) %collective-permute-start.20) | collective-permute-done | bytes 27680 | tf_op jit(solution)/shard_map/ppermute | solution.py:23
  250.4 4.3 %collective-permute-start.23 = (f32[3,18,18,1]{2,3,1,0:T(1,128)S(1)}, f32[3,18,18,1]{2,3,1,0:T(1,128)S(1)}, u32[]{:S(2)}, u32[]{:S(2)}) collective-permute-start(f32[3,18,18,1]{2,3,1,0:T(1,128)S(1)} %copy.68), channel_id=1, source_target_pairs={{0,1},{1,2},{2,3},{3,4},{4,5},{5,6},{6,7},{8,9},{9,10},{10,11},{11... | collective-permute-start | bytes 11672 | tf_op jit(solution)/shard_map/ppermute | solution.py:21
  256.7 4.2 %collective-permute-start.25 = (f32[3,1,16,128]{3,2,1,0:T(8,128)S(1)}, f32[3,1,16,128]{3,2,1,0:T(8,128)S(1)}, u32[]{:S(2)}, u32[]{:S(2)}) collective-permute-start(f32[3,1,16,128]{3,2,1,0:T(8,128)S(1)} %get-tuple-element.37), channel_id=1, source_target_pairs={{0,64},{64,128},{128,192},{192,256},{256,320},{320,384},{384,448},... | collective-permute-start | bytes 73736 | tf_op jit(solution)/shard_map/ppermute | solution.py:21
  262.8 3.2 %collective-permute-done.24 = f32[3,1,16,128]{3,2,1,0:T(8,128)S(1)} collective-permute-done((f32[3,1,16,128]{3,2,1,0:T(8,128)S(1)}, f32[3,1,16,128]{3,2,1,0:T(8,128)S(1)}, u32[]{:S(2)}, u32[]{:S(2)}) %collective-permute-start.24) | collective-permute-done | bytes 24608 | tf_op jit(solution)/shard_map/ppermute | solution.py:23
  266.1 3.4 %collective-permute-start.27 = (f32[3,18,1,128]{3,2,1,0:T(1,128)S(1)}, f32[3,18,1,128]{3,2,1,0:T(1,128)S(1)}, u32[]{:S(2)}, u32[]{:S(2)}) collective-permute-start(f32[3,18,1,128]{3,2,1,0:T(1,128)S(1)} %get-tuple-element.29), channel_id=1, source_target_pairs={{0,8},{8,16},{16,24},{24,32},{32,40},{40,48},{48,56},{1,9},{9,17},... | collective-permute-start | bytes 82952 | tf_op jit(solution)/shard_map/ppermute | solution.py:21
  270.8 3.4 %collective-permute-done.26 = f32[3,18,1,128]{3,2,1,0:T(1,128)S(1)} collective-permute-done((f32[3,18,1,128]{3,2,1,0:T(1,128)S(1)}, f32[3,18,1,128]{3,2,1,0:T(1,128)S(1)}, u32[]{:S(2)}, u32[]{:S(2)}) %collective-permute-start.26) | collective-permute-done | bytes 27680 | tf_op jit(solution)/shard_map/ppermute | solution.py:23
  276.6 4.6 %collective-permute-start.29 = (f32[3,18,18,1]{2,3,1,0:T(1,128)S(1)}, f32[3,18,18,1]{2,3,1,0:T(1,128)S(1)}, u32[]{:S(2)}, u32[]{:S(2)}) collective-permute-start(f32[3,18,18,1]{2,3,1,0:T(1,128)S(1)} %copy.72), channel_id=1, source_target_pairs={{0,1},{1,2},{2,3},{3,4},{4,5},{5,6},{6,7},{8,9},{9,10},{10,11},{11... | collective-permute-start | bytes 11672 | tf_op jit(solution)/shard_map/ppermute | solution.py:21
  (147 shorter events, 69.6 us)
Async XLA Ops:
  2.2 24.0 %all-to-all-start = ((f32[1,64,1]{2,0,1:T(1,128)}), f32[1,64,1]{2,0,1:T(1,128)S(1)}, u32[]{:S(2)}, u32[]{:S(2)}) async-start(f32[1,64,1]{2,0,1:T(1,128)} %copy.54), calls=%async_computation | async-start | bytes 65536 | tf_op jit(solution)/shard_map/all_to_all | solution.py:86
  26.2 116.1 %all-to-all-start.1 = ((f32[3,64,4096]{2,0,1:T(4,128)}), f32[3,64,4096]{2,0,1:T(4,128)}, u32[]{:S(2)}, u32[]{:S(2)}) async-start(f32[3,64,4096]{2,0,1:T(4,128)} %scatter_fusion), calls=%async_computation.1 | async-start | bytes 8388608 | tf_op jit(solution)/shard_map/all_to_all | solution.py:85
  34.5 7.2 %collective-permute-start = (bf16[3,2,16,128]{3,2,1,0:T(8,128)(2,1)S(1)}, bf16[3,2,16,128]{3,2,1,0:T(8,128)(2,1)S(1)}, u32[]{:S(2)}, u32[]{:S(2)}) collective-permute-start(bf16[3,2,16,128]{3,2,1,0:T(8,128)(2,1)S(1)} %get-tuple-element.51), channel_id=1, source_target_pairs={{0,64},{64,128},{128,192},{192,256},{256,320},{320,384},{384,448},... | collective-permute-start | bytes 73736 | tf_op jit(solution)/shard_map/ppermute | solution.py:21
  38.0 9.2 %collective-permute-start.1 = (bf16[3,2,16,128]{3,2,1,0:T(8,128)(2,1)S(1)}, bf16[3,2,16,128]{3,2,1,0:T(8,128)(2,1)S(1)}, u32[]{:S(2)}, u32[]{:S(2)}) collective-permute-start(bf16[3,2,16,128]{3,2,1,0:T(8,128)(2,1)S(1)} %get-tuple-element.50), channel_id=1, source_target_pairs={{64,0},{128,64},{192,128},{256,192},{320,256},{384,320},{448,384},... | collective-permute-start | bytes 73736 | tf_op jit(solution)/shard_map/ppermute | solution.py:23
  47.3 75.0 %collective-permute-start.2 = (bf16[3,20,2,128]{3,2,1,0:T(2,128)(2,1)S(1)}, bf16[3,20,2,128]{3,2,1,0:T(2,128)(2,1)S(1)}, u32[]{:S(2)}, u32[]{:S(2)}) collective-permute-start(bf16[3,20,2,128]{3,2,1,0:T(2,128)(2,1)S(1)} %get-tuple-element.48), channel_id=1, source_target_pairs={{0,8},{8,16},{16,24},{24,32},{32,40},{40,48},{48,56},{1,9},{9,17},... | collective-permute-start | bytes 92168 | tf_op jit(solution)/shard_map/ppermute | solution.py:21
  48.9 77.7 %collective-permute-start.3 = (bf16[3,20,2,128]{3,2,1,0:T(2,128)(2,1)S(1)}, bf16[3,20,2,128]{3,2,1,0:T(2,128)(2,1)S(1)}, u32[]{:S(2)}, u32[]{:S(2)}) collective-permute-start(bf16[3,20,2,128]{3,2,1,0:T(2,128)(2,1)S(1)} %get-tuple-element.49), channel_id=1, source_target_pairs={{8,0},{16,8},{24,16},{32,24},{40,32},{48,40},{56,48},{9,1},{17,9},... | collective-permute-start | bytes 92168 | tf_op jit(solution)/shard_map/ppermute | solution.py:23
  126.9 9.9 %collective-permute-start.4 = (bf16[3,20,20,2]{3,2,1,0:T(8,128)(2,1)S(1)}, bf16[3,20,20,2]{3,2,1,0:T(8,128)(2,1)S(1)}, u32[]{:S(2)}, u32[]{:S(2)}) collective-permute-start(bf16[3,20,20,2]{3,2,1,0:T(8,128)(2,1)S(1)} %get-tuple-element.46), channel_id=1, source_target_pairs={{0,1},{1,2},{2,3},{3,4},{4,5},{5,6},{6,7},{8,9},{9,10},{10,11},{11... | collective-permute-start | bytes 14408 | tf_op jit(solution)/shard_map/ppermute | solution.py:21
  130.2 10.6 %collective-permute-start.5 = (bf16[3,20,20,2]{3,2,1,0:T(8,128)(2,1)S(1)}, bf16[3,20,20,2]{3,2,1,0:T(8,128)(2,1)S(1)}, u32[]{:S(2)}, u32[]{:S(2)}) collective-permute-start(bf16[3,20,20,2]{3,2,1,0:T(8,128)(2,1)S(1)} %get-tuple-element.47), channel_id=1, source_target_pairs={{1,0},{2,1},{3,2},{4,3},{5,4},{6,5},{7,6},{9,8},{10,9},{11,10},{12... | collective-permute-start | bytes 14408 | tf_op jit(solution)/shard_map/ppermute | solution.py:23
  160.5 9.3 %collective-permute-start.7 = (f32[3,1,16,128]{3,2,1,0:T(8,128)S(1)}, f32[3,1,16,128]{3,2,1,0:T(8,128)S(1)}, u32[]{:S(2)}, u32[]{:S(2)}) collective-permute-start(f32[3,1,16,128]{3,2,1,0:T(8,128)S(1)} %get-tuple-element.45), channel_id=1, source_target_pairs={{0,64},{64,128},{128,192},{192,256},{256,320},{320,384},{384,448},... | collective-permute-start | bytes 73736 | tf_op jit(solution)/shard_map/ppermute | solution.py:21
  168.0 5.1 %collective-permute-start.6 = (f32[3,1,16,128]{3,2,1,0:T(8,128)S(1)}, f32[3,1,16,128]{3,2,1,0:T(8,128)S(1)}, u32[]{:S(2)}, u32[]{:S(2)}) collective-permute-start(f32[3,1,16,128]{3,2,1,0:T(8,128)S(1)} %get-tuple-element.44), channel_id=1, source_target_pairs={{64,0},{128,64},{192,128},{256,192},{320,256},{384,320},{448,384},... | collective-permute-start | bytes 73736 | tf_op jit(solution)/shard_map/ppermute | solution.py:23
  173.2 3.4 %collective-permute-start.9 = (f32[3,18,1,128]{3,2,1,0:T(1,128)S(1)}, f32[3,18,1,128]{3,2,1,0:T(1,128)S(1)}, u32[]{:S(2)}, u32[]{:S(2)}) collective-permute-start(f32[3,18,1,128]{3,2,1,0:T(1,128)S(1)} %get-tuple-element.35), channel_id=1, source_target_pairs={{0,8},{8,16},{16,24},{24,32},{32,40},{40,48},{48,56},{1,9},{9,17},... | collective-permute-start | bytes 82952 | tf_op jit(solution)/shard_map/ppermute | solution.py:21
  175.3 5.0 %collective-permute-start.8 = (f32[3,18,1,128]{3,2,1,0:T(1,128)S(1)}, f32[3,18,1,128]{3,2,1,0:T(1,128)S(1)}, u32[]{:S(2)}, u32[]{:S(2)}) collective-permute-start(f32[3,18,1,128]{3,2,1,0:T(1,128)S(1)} %get-tuple-element.36), channel_id=1, source_target_pairs={{8,0},{16,8},{24,16},{32,24},{40,32},{48,40},{56,48},{9,1},{17,9},... | collective-permute-start | bytes 82952 | tf_op jit(solution)/shard_map/ppermute | solution.py:23
  182.1 9.1 %collective-permute-start.11 = (f32[3,18,18,1]{2,3,1,0:T(1,128)S(1)}, f32[3,18,18,1]{2,3,1,0:T(1,128)S(1)}, u32[]{:S(2)}, u32[]{:S(2)}) collective-permute-start(f32[3,18,18,1]{2,3,1,0:T(1,128)S(1)} %copy.60), channel_id=1, source_target_pairs={{0,1},{1,2},{2,3},{3,4},{4,5},{5,6},{6,7},{8,9},{9,10},{10,11},{11... | collective-permute-start | bytes 11672 | tf_op jit(solution)/shard_map/ppermute | solution.py:21
  185.4 5.5 %collective-permute-start.10 = (f32[3,18,18,1]{2,3,1,0:T(1,128)S(1)}, f32[3,18,18,1]{2,3,1,0:T(1,128)S(1)}, u32[]{:S(2)}, u32[]{:S(2)}) collective-permute-start(f32[3,18,18,1]{2,3,1,0:T(1,128)S(1)} %copy.58), channel_id=1, source_target_pairs={{1,0},{2,1},{3,2},{4,3},{5,4},{6,5},{7,6},{9,8},{10,9},{11,10},{12... | collective-permute-start | bytes 11672 | tf_op jit(solution)/shard_map/ppermute | solution.py:23
  194.3 6.3 %collective-permute-start.13 = (f32[3,1,16,128]{3,2,1,0:T(8,128)S(1)}, f32[3,1,16,128]{3,2,1,0:T(8,128)S(1)}, u32[]{:S(2)}, u32[]{:S(2)}) collective-permute-start(f32[3,1,16,128]{3,2,1,0:T(8,128)S(1)} %get-tuple-element.41), channel_id=1, source_target_pairs={{0,64},{64,128},{128,192},{192,256},{256,320},{320,384},{384,448},... | collective-permute-start | bytes 73736 | tf_op jit(solution)/shard_map/ppermute | solution.py:21
  198.7 5.1 %collective-permute-start.12 = (f32[3,1,16,128]{3,2,1,0:T(8,128)S(1)}, f32[3,1,16,128]{3,2,1,0:T(8,128)S(1)}, u32[]{:S(2)}, u32[]{:S(2)}) collective-permute-start(f32[3,1,16,128]{3,2,1,0:T(8,128)S(1)} %get-tuple-element.42), channel_id=1, source_target_pairs={{64,0},{128,64},{192,128},{256,192},{320,256},{384,320},{448,384},... | collective-permute-start | bytes 73736 | tf_op jit(solution)/shard_map/ppermute | solution.py:23
  203.9 6.5 %collective-permute-start.15 = (f32[3,18,1,128]{3,2,1,0:T(1,128)S(1)}, f32[3,18,1,128]{3,2,1,0:T(1,128)S(1)}, u32[]{:S(2)}, u32[]{:S(2)}) collective-permute-start(f32[3,18,1,128]{3,2,1,0:T(1,128)S(1)} %get-tuple-element.33), channel_id=1, source_target_pairs={{0,8},{8,16},{16,24},{24,32},{32,40},{40,48},{48,56},{1,9},{9,17},... | collective-permute-start | bytes 82952 | tf_op jit(solution)/shard_map/ppermute | solution.py:21
  208.4 4.9 %collective-permute-start.14 = (f32[3,18,1,128]{3,2,1,0:T(1,128)S(1)}, f32[3,18,1,128]{3,2,1,0:T(1,128)S(1)}, u32[]{:S(2)}, u32[]{:S(2)}) collective-permute-start(f32[3,18,1,128]{3,2,1,0:T(1,128)S(1)} %get-tuple-element.34), channel_id=1, source_target_pairs={{8,0},{16,8},{24,16},{32,24},{40,32},{48,40},{56,48},{9,1},{17,9},... | collective-permute-start | bytes 82952 | tf_op jit(solution)/shard_map/ppermute | solution.py:23
  214.5 9.9 %collective-permute-start.17 = (f32[3,18,18,1]{2,3,1,0:T(1,128)S(1)}, f32[3,18,18,1]{2,3,1,0:T(1,128)S(1)}, u32[]{:S(2)}, u32[]{:S(2)}) collective-permute-start(f32[3,18,18,1]{2,3,1,0:T(1,128)S(1)} %copy.64), channel_id=1, source_target_pairs={{0,1},{1,2},{2,3},{3,4},{4,5},{5,6},{6,7},{8,9},{9,10},{10,11},{11... | collective-permute-start | bytes 11672 | tf_op jit(solution)/shard_map/ppermute | solution.py:21
  219.1 4.9 %collective-permute-start.16 = (f32[3,18,18,1]{2,3,1,0:T(1,128)S(1)}, f32[3,18,18,1]{2,3,1,0:T(1,128)S(1)}, u32[]{:S(2)}, u32[]{:S(2)}) collective-permute-start(f32[3,18,18,1]{2,3,1,0:T(1,128)S(1)} %copy.62), channel_id=1, source_target_pairs={{1,0},{2,1},{3,2},{4,3},{5,4},{6,5},{7,6},{9,8},{10,9},{11,10},{12... | collective-permute-start | bytes 11672 | tf_op jit(solution)/shard_map/ppermute | solution.py:23
  229.6 6.3 %collective-permute-start.19 = (f32[3,1,16,128]{3,2,1,0:T(8,128)S(1)}, f32[3,1,16,128]{3,2,1,0:T(8,128)S(1)}, u32[]{:S(2)}, u32[]{:S(2)}) collective-permute-start(f32[3,1,16,128]{3,2,1,0:T(8,128)S(1)} %get-tuple-element.39), channel_id=1, source_target_pairs={{0,64},{64,128},{128,192},{192,256},{256,320},{320,384},{384,448},... | collective-permute-start | bytes 73736 | tf_op jit(solution)/shard_map/ppermute | solution.py:21
  233.9 5.1 %collective-permute-start.18 = (f32[3,1,16,128]{3,2,1,0:T(8,128)S(1)}, f32[3,1,16,128]{3,2,1,0:T(8,128)S(1)}, u32[]{:S(2)}, u32[]{:S(2)}) collective-permute-start(f32[3,1,16,128]{3,2,1,0:T(8,128)S(1)} %get-tuple-element.40), channel_id=1, source_target_pairs={{64,0},{128,64},{192,128},{256,192},{320,256},{384,320},{448,384},... | collective-permute-start | bytes 73736 | tf_op jit(solution)/shard_map/ppermute | solution.py:23
  239.1 5.4 %collective-permute-start.21 = (f32[3,18,1,128]{3,2,1,0:T(1,128)S(1)}, f32[3,18,1,128]{3,2,1,0:T(1,128)S(1)}, u32[]{:S(2)}, u32[]{:S(2)}) collective-permute-start(f32[3,18,1,128]{3,2,1,0:T(1,128)S(1)} %get-tuple-element.31), channel_id=1, source_target_pairs={{0,8},{8,16},{16,24},{24,32},{32,40},{40,48},{48,56},{1,9},{9,17},... | collective-permute-start | bytes 82952 | tf_op jit(solution)/shard_map/ppermute | solution.py:21
  243.2 4.7 %collective-permute-start.20 = (f32[3,18,1,128]{3,2,1,0:T(1,128)S(1)}, f32[3,18,1,128]{3,2,1,0:T(1,128)S(1)}, u32[]{:S(2)}, u32[]{:S(2)}) collective-permute-start(f32[3,18,1,128]{3,2,1,0:T(1,128)S(1)} %get-tuple-element.32), channel_id=1, source_target_pairs={{8,0},{16,8},{24,16},{32,24},{40,32},{48,40},{56,48},{9,1},{17,9},... | collective-permute-start | bytes 82952 | tf_op jit(solution)/shard_map/ppermute | solution.py:23
  248.7 6.0 %collective-permute-start.22 = (f32[3,18,18,1]{2,3,1,0:T(1,128)S(1)}, f32[3,18,18,1]{2,3,1,0:T(1,128)S(1)}, u32[]{:S(2)}, u32[]{:S(2)}) collective-permute-start(f32[3,18,18,1]{2,3,1,0:T(1,128)S(1)} %copy.66), channel_id=1, source_target_pairs={{1,0},{2,1},{3,2},{4,3},{5,4},{6,5},{7,6},{9,8},{10,9},{11,10},{12... | collective-permute-start | bytes 11672 | tf_op jit(solution)/shard_map/ppermute | solution.py:23
  250.4 5.2 %collective-permute-start.23 = (f32[3,18,18,1]{2,3,1,0:T(1,128)S(1)}, f32[3,18,18,1]{2,3,1,0:T(1,128)S(1)}, u32[]{:S(2)}, u32[]{:S(2)}) collective-permute-start(f32[3,18,18,1]{2,3,1,0:T(1,128)S(1)} %copy.68), channel_id=1, source_target_pairs={{0,1},{1,2},{2,3},{3,4},{4,5},{5,6},{6,7},{8,9},{9,10},{10,11},{11... | collective-permute-start | bytes 11672 | tf_op jit(solution)/shard_map/ppermute | solution.py:21
  256.7 6.1 %collective-permute-start.25 = (f32[3,1,16,128]{3,2,1,0:T(8,128)S(1)}, f32[3,1,16,128]{3,2,1,0:T(8,128)S(1)}, u32[]{:S(2)}, u32[]{:S(2)}) collective-permute-start(f32[3,1,16,128]{3,2,1,0:T(8,128)S(1)} %get-tuple-element.37), channel_id=1, source_target_pairs={{0,64},{64,128},{128,192},{192,256},{256,320},{320,384},{384,448},... | collective-permute-start | bytes 73736 | tf_op jit(solution)/shard_map/ppermute | solution.py:21
  260.9 5.1 %collective-permute-start.24 = (f32[3,1,16,128]{3,2,1,0:T(8,128)S(1)}, f32[3,1,16,128]{3,2,1,0:T(8,128)S(1)}, u32[]{:S(2)}, u32[]{:S(2)}) collective-permute-start(f32[3,1,16,128]{3,2,1,0:T(8,128)S(1)} %get-tuple-element.38), channel_id=1, source_target_pairs={{64,0},{128,64},{192,128},{256,192},{320,256},{384,320},{448,384},... | collective-permute-start | bytes 73736 | tf_op jit(solution)/shard_map/ppermute | solution.py:23
  266.1 4.7 %collective-permute-start.27 = (f32[3,18,1,128]{3,2,1,0:T(1,128)S(1)}, f32[3,18,1,128]{3,2,1,0:T(1,128)S(1)}, u32[]{:S(2)}, u32[]{:S(2)}) collective-permute-start(f32[3,18,1,128]{3,2,1,0:T(1,128)S(1)} %get-tuple-element.29), channel_id=1, source_target_pairs={{0,8},{8,16},{16,24},{24,32},{32,40},{40,48},{48,56},{1,9},{9,17},... | collective-permute-start | bytes 82952 | tf_op jit(solution)/shard_map/ppermute | solution.py:21
  269.5 4.7 %collective-permute-start.26 = (f32[3,18,1,128]{3,2,1,0:T(1,128)S(1)}, f32[3,18,1,128]{3,2,1,0:T(1,128)S(1)}, u32[]{:S(2)}, u32[]{:S(2)}) collective-permute-start(f32[3,18,1,128]{3,2,1,0:T(1,128)S(1)} %get-tuple-element.30), channel_id=1, source_target_pairs={{8,0},{16,8},{24,16},{32,24},{40,32},{48,40},{56,48},{9,1},{17,9},... | collective-permute-start | bytes 82952 | tf_op jit(solution)/shard_map/ppermute | solution.py:23
  274.9 6.3 %collective-permute-start.28 = (f32[3,18,18,1]{2,3,1,0:T(1,128)S(1)}, f32[3,18,18,1]{2,3,1,0:T(1,128)S(1)}, u32[]{:S(2)}, u32[]{:S(2)}) collective-permute-start(f32[3,18,18,1]{2,3,1,0:T(1,128)S(1)} %copy.70), channel_id=1, source_target_pairs={{1,0},{2,1},{3,2},{4,3},{5,4},{6,5},{7,6},{9,8},{10,9},{11,10},{12... | collective-permute-start | bytes 11672 | tf_op jit(solution)/shard_map/ppermute | solution.py:23
  276.6 5.6 %collective-permute-start.29 = (f32[3,18,18,1]{2,3,1,0:T(1,128)S(1)}, f32[3,18,18,1]{2,3,1,0:T(1,128)S(1)}, u32[]{:S(2)}, u32[]{:S(2)}) collective-permute-start(f32[3,18,18,1]{2,3,1,0:T(1,128)S(1)} %copy.72), channel_id=1, source_target_pairs={{0,1},{1,2},{2,3},{3,4},{4,5},{5,6},{6,7},{8,9},{9,10},{10,11},{11... | collective-permute-start | bytes 11672 | tf_op jit(solution)/shard_map/ppermute | solution.py:21
  (23 other events, 392.4 us)
where the time goes:
time: 289 us; the launch traced here: 284 us
  waiting for transfers between devices  125 us (43%)
  starting transfers between devices  103 us (36%)
  local copies, waits for them, and re-layouts  38 us (13%)
  other arithmetic  16.9 us (6%)
    ppermute x15, waiting for transfers between devices, extended(): lax.ppermute(tail, axis, [(i, (i + 1) % count) for i in range(ends)])  79.1 us
    ppermute x15, starting transfers between devices, extended(): lax.ppermute(tail, axis, [(i, (i + 1) % count) for i in range(ends)])  57.5 us
    ppermute x15, waiting for transfers between devices, extended(): lax.ppermute(head, axis, [((i + 1) % count, i) for i in range(ends)])  43.7 us
    ppermute x15, starting transfers between devices, extended(): lax.ppermute(head, axis, [((i + 1) % count, i) for i in range(ends)])  22.5 us
    all_to_all x1, starting transfers between devices, body(): lax.all_to_all(labels, ('stream', 'span'), split_axis=1, concat_axis=1, t...  14.8 us
    all_to_all x1, starting transfers between devices, body(): lax.all_to_all(outgoing, ('stream', 'span'), split_axis=1, concat_axis=1,...  8.29 us
    scatter x2, local copies, waits for them, and re-layouts, body(): placed = jnp.zeros((3, block_count, block_cells), jnp.float32).at[:, inco...  7.68 us
    reduce_sum x2, other arithmetic, advect(): jnp.sum(current * slopes[axis_num], axis=0)  6.3 us
  transfers between devices with their start and end apart: 32, of which 19 were waited for; matrix products, arithmetic and copies ran while one was open for 6% of the time, Pallas kernels for 0%

commit v1 on v0

v1 whole, which is shorter than its diff:
```python
import functools

import jax
import jax.numpy as jnp
from jax import lax
from jax.experimental import pallas as pl
from jax.experimental.pallas import tpu as pltpu
from jax.sharding import PartitionSpec as P

SECTIONS = 2
ADVECT = 0.1
DIFFUSE = 0.1
LEVELS = 32767.0

RING = 8
CHIPS = 4
SLOTS = 8
EDGE = 16
TILES = 32
MESH = pl.DeviceIdType.MESH


def lanes_of(shape):
    return lax.broadcasted_iota(jnp.int32, shape, len(shape) - 1)


def rows_of(shape):
    return lax.broadcasted_iota(jnp.int32, shape, len(shape) - 2)


def swap_groups(tile):
    row, group = rows_of(tile.shape), lanes_of(tile.shape) // EDGE
    for bit in (1, 2, 4):
        row_bit, group_bit = (row & bit) != 0, (group & bit) != 0
        down = pltpu.roll(pltpu.roll(tile, bit, 0), 128 - EDGE * bit, 1)
        if bit == 4:
            up = down
        else:
            up = pltpu.roll(pltpu.roll(tile, 8 - bit, 0), EDGE * bit, 1)
        tile = jnp.where(row_bit == group_bit, tile, jnp.where(row_bit, down, up))
    return tile


def pack_ends(tiles):
    pair = ((lanes_of((8, 128)) + 1) & 127) // 2
    shift = 1
    while len(tiles) > 1:
        later = (pair & shift) != 0
        tiles = [
            jnp.where(later, pltpu.roll(b, 2 * shift, 1), a)
            for a, b in zip(tiles[0::2], tiles[1::2])
        ]
        shift *= 2
    return tiles[0]


def kernel(
    target, fish, forcing, old, velocity, chi, out,
    gathered, meta, staged, outgoing, out_scales, incoming, in_scales, decoded,
    found, found_s, fields, face_y, halo_y, face_z, halo_z, slopes, weight, pull,
    send_sems, recv_sems, local_sem,
):
    stream, span, depth = (lax.axis_index(a) for a in ("stream", "span", "depth"))
    chip, core = stream // 2, stream % 2
    other_core = {"stream": chip * 2 + 1 - core}

    def along(axis, index, step):
        return {axis: (index + step + RING) % RING}

    copies = {}

    def send(key, src, dst, device):
        number = len(copies)
        copy = pltpu.make_async_remote_copy(
            src_ref=src,
            dst_ref=dst,
            send_sem=send_sems.at[number],
            recv_sem=recv_sems.at[number],
            device_id=device,
            device_id_type=MESH,
        )
        copies[key] = copy
        copy.start()

    barrier = pltpu.get_barrier_semaphore()
    partners = [along("span", span, 1), along("span", span, -1)]
    partners += [along("depth", depth, 1), along("depth", depth, -1)]
    partners += [along("stream", stream, s) for s in (1, -1, 2, 4, 6)]
    for partner in partners:
        pl.semaphore_signal(barrier, inc=1, device_id=partner, device_id_type=MESH)

    for c in range(3):
        top = jnp.abs(old[c, :, 0:128])
        for t in range(1, TILES):
            top = jnp.maximum(top, jnp.abs(old[c, :, 128 * t : 128 * t + 128]))
        meta[0, c] = top * (1.0 / LEVELS)
        inverse = LEVELS / jnp.maximum(top, 1e-30)
        for t in range(TILES):
            staged[c][pl.ds(t, SLOTS, stride=TILES), :] = jnp.round(
                old[c, :, 128 * t : 128 * t + 128] * inverse
            )
        for b in range(SLOTS):
            codes = staged[c][TILES * b : TILES * (b + 1), :]
            gathered[c][b] = codes.astype(jnp.int32).astype(jnp.int16)
    label = jnp.zeros((8, 128), jnp.int32)
    for b in range(SLOTS):
        label = jnp.where(rows_of((8, 128)) == b, target[b], label)
    meta[0, 3] = label.astype(jnp.float32)

    pl.semaphore_wait(barrier, len(partners))

    def places(kind, e, part):
        if kind == 3:
            return meta.at[e]
        if part is None:
            return gathered[kind].at[pl.ds(8 * e, 8)]
        return gathered[kind].at[pl.ds(8 * e + 4 * part, 4)]

    def hop_right(kind, hop):
        part = 0 if hop == 4 and kind < 3 else None
        send(("r", kind, hop), places(kind, hop - 1, part), places(kind, hop, part), along("span", span, 1))

    def hop_left(kind, hop):
        part = 1 if hop == 4 else None
        send(("l", kind, hop), places(kind, (9 - hop) % 8, part), places(kind, 8 - hop, part), along("span", span, -1))

    def to_core(kind, e, part=None):
        send(("c", kind, e, part), places(kind, e, part), places(kind, 8 + e, part), other_core)

    kinds = (3, 0, 1, 2)
    for kind in kinds:
        hop_right(kind, 1)
        hop_left(kind, 1)
    for kind in kinds:
        to_core(kind, 0)

    def keep_faces(n, i, c, value):
        face_y[n][0, i * 3 + c : i * 3 + c + 1, :] = value[0:1]
        face_y[n][1, i * 3 + c : i * 3 + c + 1, :] = value[EDGE - 1 : EDGE]

    def keep_ends(n, tiles):
        for c in range(3):
            face_z[n][c] = pack_ends(tiles[c])

    def start_halo(n):
        field = fields[n]
        send((n, "x", 0), field.at[pl.ds(48, 3)], field.at[pl.ds(0, 3)], along("stream", stream, 1))
        send((n, "x", 1), field.at[pl.ds(3, 3)], field.at[pl.ds(51, 3)], along("stream", stream, -1))
        send((n, "y", 0), face_y[n].at[1], halo_y[n].at[0], along("span", span, 1))
        send((n, "y", 1), face_y[n].at[0], halo_y[n].at[1], along("span", span, -1))
        send((n, "z", 0), face_z[n], halo_z[n].at[0], along("depth", depth, 1))
        send((n, "z", 1), face_z[n], halo_z[n].at[1], along("depth", depth, -1))

    def finish_halo(n):
        for axis in ("x", "y", "z"):
            for side in (0, 1):
                copies[(n, axis, side)].wait_recv()

        @pl.when(stream == 0)
        def _():
            fields[n][0:3] = jnp.zeros((3, EDGE, 128), jnp.float32)

        @pl.when(stream == RING - 1)
        def _():
            fields[n][51:54] = jnp.zeros((3, EDGE, 128), jnp.float32)

        @pl.when(span == 0)
        def _():
            halo_y[n][0] = jnp.zeros((48, 128), jnp.float32)

        @pl.when(span == RING - 1)
        def _():
            halo_y[n][1] = jnp.zeros((48, 128), jnp.float32)

        ends = []
        odd = (lanes_of((8, 128)) & 1) == 1
        for c in range(3):
            before = jnp.where(depth == 0, 0.0, pltpu.roll(halo_z[n][0, c], 1, 1))
            after = jnp.where(depth == RING - 1, 0.0, pltpu.roll(halo_z[n][1, c], 127, 1))
            ends.append(jnp.where(odd, after, before))
        return ends

    wide = (EDGE, 128)

    def around(n, ends, i, c):
        here = fields[n][(i + 1) * 3 + c]
        row, lane = rows_of(wide), lanes_of(wide)
        at = i * 3 + c
        y_before = jnp.where(row == 0, halo_y[n][0, at : at + 1, :], pltpu.roll(here, 1, 0))
        y_after = jnp.where(row == EDGE - 1, halo_y[n][1, at : at + 1, :], pltpu.roll(here, EDGE - 1, 0))
        end = jnp.concatenate(
            [pltpu.roll(ends[c], (128 - 2 * v) % 128, 1) for v in (2 * i, 2 * i + 1)], axis=0
        )
        z_before = jnp.where(lane == 0, end, pltpu.roll(here, 1, 1))
        z_after = jnp.where(lane == 127, end, pltpu.roll(here, 127, 1))
        return here, fields[n][i * 3 + c], fields[n][(i + 2) * 3 + c], y_before, y_after, z_before, z_after

    tiles = [[], [], []]
    for i in range(EDGE):
        for c in range(3):
            value = velocity[c, i].astype(jnp.float32)
            fields[4][(i + 1) * 3 + c] = value
            keep_faces(4, i, c, value)
            tiles[c] += [value[0:8], value[8:16]]
    keep_ends(4, tiles)
    start_halo(4)

    def forward(kind, hop):
        copies[("r", kind, hop)].wait_recv()
        if hop < 4:
            hop_right(kind, hop + 1)
        if hop < 4 or kind == 3:
            to_core(kind, hop)
        else:
            to_core(kind, hop, 0)
        if hop == 4 and kind == 3:
            return
        copies[("l", kind, hop)].wait_recv()
        if hop < 3 or kind < 3 and hop == 3:
            hop_left(kind, hop + 1)
        if hop < 4:
            to_core(kind, 8 - hop)
        else:
            to_core(kind, 4, 1)

    for kind in kinds:
        forward(kind, 1)

    ends = finish_halo(4)
    for i in range(EDGE):
        for k in range(3):
            _, *near = around(4, ends, i, k)
            for axis in range(3):
                slopes[(axis * 3 + k) * EDGE + i] = ADVECT * (near[2 * axis + 1] - near[2 * axis])

    for kind in kinds:
        forward(kind, 2)

    group = lanes_of(wide) // EDGE
    forces = []
    for c in range(3):
        force = jnp.zeros(wide, jnp.float32)
        for b in range(SLOTS):
            force = jnp.where(group == b, forcing[fish[0, 0, b], c], force)
        forces.append(force)
    for i in range(EDGE):
        level = chi[i]
        share = 1.0 / (1.0 + level)
        weight[i] = share
        for c in range(3):
            pull[i * 3 + c] = level * share * forces[c]

    for kind in kinds:
        forward(kind, 3)
    forward(3, 4)
    for e in range(8):
        copies[("c", 3, e, None)].wait_recv()

    shape = (8, 128)
    lane, row = lanes_of(shape), rows_of(shape)
    owner = (2 * ((chip + lane // 8) % CHIPS) + core) * RING + span
    wanted = jnp.where(lane < CHIPS * SLOTS, owner * SLOTS + lane % 8, -1).astype(jnp.float32)
    at = jnp.zeros(shape, jnp.float32)
    for e in range(16):
        at = at + jnp.where(meta[e, 3] == wanted, (row + (8 * e + 1)).astype(jnp.float32), 0.0)
    found[...] = jnp.broadcast_to(jnp.sum(at, axis=0, keepdims=True), shape).astype(jnp.int32)
    copy = pltpu.make_async_copy(found, found_s, local_sem)
    copy.start()
    copy.wait()
    where_from = []
    for q in range(CHIPS * SLOTS):
        k, j = q // SLOTS, q % SLOTS
        code = found_s[0, q]
        block = jnp.minimum(jnp.maximum(code - 1, 0), 127)
        where_from.append(block)
        valid = jnp.where(code > 0, 1.0, 0.0)
        for c in range(3):
            scale = meta[block // 8, c, pl.ds(block % 8, 1), :] * valid
            if k == 0:
                in_scales[0, c, j : j + 1, :] = scale
            else:
                out_scales[k - 1, c, j : j + 1, :] = scale
    for k in (2, 1, 3):
        send(("s", k), out_scales.at[k - 1], in_scales.at[k], along("stream", stream, 2 * k))

    for kind in (0, 1, 2):
        forward(kind, 4)
        for e in range(8):
            for part in (0, 1) if e == 4 else (None,):
                copies[("c", kind, e, part)].wait_recv()
        for k in (2, 1, 3, 0):
            for j in range(SLOTS):
                block = gathered[kind][where_from[k * SLOTS + j]]
                if k == 0:
                    incoming[kind][0, j] = block
                else:
                    outgoing[kind][k - 1, j] = block
            if k:
                send(("x", kind, k), outgoing[kind].at[k - 1], incoming[kind].at[k], along("stream", stream, 2 * k))

    for k in (2, 1, 3):
        copies[("s", k)].wait_recv()
    tiles = [[], [], []]
    for c in range(3):
        for k in (2, 1, 3):
            copies[("x", c, k)].wait_recv()
        for j in range(SLOTS):
            total = incoming[c][0, j].astype(jnp.float32) * in_scales[0, c, j : j + 1, :]
            for k in range(1, CHIPS):
                total = total + incoming[c][k, j].astype(jnp.float32) * in_scales[k, c, j : j + 1, :]
            decoded[c][TILES * j : TILES * (j + 1), :] = total
        for i in range(EDGE):
            halves = [swap_groups(decoded[c][pl.ds(2 * i + h, SLOTS, stride=TILES), :]) for h in (0, 1)]
            for h in (0, 1):
                fields[0][(i + 1) * 3 + c, 8 * h : 8 * h + 8, :] = halves[h]
            face_y[0][0, i * 3 + c : i * 3 + c + 1, :] = halves[0][0:1]
            face_y[0][1, i * 3 + c : i * 3 + c + 1, :] = halves[1][7:8]
            tiles[c] += halves
    keep_ends(0, tiles)

    for section in range(SECTIONS):
        n = 2 * section
        start_halo(n)
        ends = finish_halo(n)
        tiles = [[], [], []]
        for i in range(EDGE):
            near = [around(n, ends, i, c) for c in range(3)]
            carried = [ADVECT * fields[4][(i + 1) * 3 + k] for k in range(3)]
            for c in range(3):
                value = near[c][0]
                for k in range(3):
                    value = value + carried[k] * (near[c][2 * k + 2] - near[c][2 * k + 1])
                    value = value - near[k][0] * slopes[(c * 3 + k) * EDGE + i]
                fields[n + 1][(i + 1) * 3 + c] = value
                keep_faces(n + 1, i, c, value)
                tiles[c] += [value[0:8], value[8:16]]
        keep_ends(n + 1, tiles)
        start_halo(n + 1)
        ends = finish_halo(n + 1)
        tiles = [[], [], []]
        for i in range(EDGE):
            share = weight[i]
            for c in range(3):
                here, *near = around(n + 1, ends, i, c)
                total = (near[0] + near[1]) + (near[2] + near[3]) + (near[4] + near[5])
                value = (here + DIFFUSE * (total - 6.0 * here)) * share + pull[i * 3 + c]
                if section == SECTIONS - 1:
                    out[c, i] = value
                else:
                    fields[n + 2][(i + 1) * 3 + c] = value
                    keep_faces(n + 2, i, c, value)
                    tiles[c] += [value[0:8], value[8:16]]
        if section < SECTIONS - 1:
            keep_ends(n + 2, tiles)

    for copy in copies.values():
        copy.wait_send()


def body(old_adjoint, target, velocity, chi, fish, fish_forcing):
    f32, i16 = jnp.float32, jnp.int16
    v = pltpu.VMEM
    scratch = [
        [v((128, TILES, 128), i16)] * 3,
        v((16, 4, 8, 128), f32),
        [v((SLOTS * TILES, 128), f32)] * 3,
        [v((CHIPS - 1, SLOTS, TILES, 128), i16)] * 3,
        v((CHIPS - 1, 3, SLOTS, 128), f32),
        [v((CHIPS, SLOTS, TILES, 128), i16)] * 3,
        v((CHIPS, 3, SLOTS, 128), f32),
        [v((SLOTS * TILES, 128), f32)] * 3,
        v((8, 128), jnp.int32),
        pltpu.SMEM((8, 128), jnp.int32),
        [v((18 * 3, EDGE, 128), f32)] * 5,
        [v((2, 48, 128), f32)] * 5,
        [v((2, 48, 128), f32)] * 5,
        [v((3, 8, 128), f32)] * 5,
        [v((2, 3, 8, 128), f32)] * 5,
        v((9 * EDGE, EDGE, 128), f32),
        v((EDGE, EDGE, 128), f32),
        v((3 * EDGE, EDGE, 128), f32),
        pltpu.SemaphoreType.DMA((128,)),
        pltpu.SemaphoreType.DMA((128,)),
        pltpu.SemaphoreType.DMA,
    ]
    smem = pl.BlockSpec(memory_space=pltpu.SMEM)
    vmem = pl.BlockSpec(memory_space=pltpu.VMEM)
    return pl.pallas_call(
        kernel,
        out_shape=jax.ShapeDtypeStruct(velocity.shape, f32),
        in_specs=[smem, smem, smem, vmem, vmem, vmem],
        out_specs=vmem,
        scratch_shapes=scratch,
        compiler_params=pltpu.CompilerParams(
            collective_id=0, has_side_effects=True, vmem_limit_bytes=40 * 1024 * 1024
        ),
    )(target, fish, fish_forcing, old_adjoint, velocity, chi)


def solution(mesh):
    return jax.shard_map(
        body,
        mesh=mesh,
        in_specs=(
            P(None, ("stream", "span", "depth"), None),
            P(("stream", "span", "depth")),
            P(None, "stream", "span", "depth"),
            P("stream", "span", "depth"),
            P("stream", "span", "depth"),
            P(),
        ),
        out_specs=P(None, "stream", "span", "depth"),
        check_vma=False,
    )
```

time: 289 us -> 68.6 us (0.24); the launches traced: 284 us -> 68.4 us
  waiting for transfers between devices: 125 us -> 0 us
  starting transfers between devices: 103 us -> 0 us
  Pallas kernels: 0 us -> 64 us
  local copies, waits for them, and re-layouts: 38 us -> 4.37 us
  other arithmetic: 16.9 us -> 0 us
    ppermute x30 -> x0, waiting for transfers between devices: 123 us -> none  [the longest x15 79.1 us: extended(): lax.ppermute(tail, axis, [(i, (i + 1) % count) for i in range(ends)])]
    ppermute x30 -> x0, starting transfers between devices: 80 us -> none  [the longest x15 57.5 us: extended(): lax.ppermute(tail, axis, [(i, (i + 1) % count) for i in range(ends)])]
    pallas_call x0 -> x1, Pallas kernels: none -> 64 us  [body(): pl.pallas_call(kernel, out_shape=jax.ShapeDtypeStruct(velocity.shape, f32...]
    all_to_all x2 -> x0, starting transfers between devices: 23.1 us -> none  [the longest x1 14.8 us: body(): lax.all_to_all(labels, ('stream', 'span'), split_axis=1, concat_axis=1, t...]
    scatter x4 -> x0, local copies, waits for them, and re-layouts: 10.8 us -> none  [the longest x2 7.68 us: body(): placed = jnp.zeros((3, block_count, block_cells), jnp.float32).at[:, inco...]
    reduce_sum x3 -> x0, other arithmetic: 6.48 us -> none  [the longest x2 6.3 us: advect(): jnp.sum(current * slopes[axis_num], axis=0)]
    slice x21 -> x0, local copies, waits for them, and re-layouts: 6.45 us -> none  [the longest x10 2.66 us: extended(): head = lax.slice_in_dim(cells, 0, width, axis=dim)]
    transpose x1 -> x0, local copies, waits for them, and re-layouts: 5.39 us -> none  [body(): adjoint = adjoint.transpose(0, 1, 4, 2, 5, 3, 6).reshape(velocity.shape)]
  transfers between devices with their start and end apart: 32 -> 0, of which waited for: 19 -> 0; matrix products, arithmetic and copies ran while one was open for 6% -> 0% of each run, Pallas kernels for 0% -> 0%
where the time goes in v1:
time: 68.6 us; the launch traced here: 68.4 us
  Pallas kernels  64 us (93%)
  local copies, waits for them, and re-layouts  4.37 us (6%)
    pallas_call x1, Pallas kernels, body(): pl.pallas_call(kernel, out_shape=jax.ShapeDtypeStruct(velocity.shape, f32...  64 us
    unnamed x12, local copies, waits for them, and re-layouts  4.37 us

profile of v1, /device:TPU:1, one launch (start us, length us, event | category | flops | bytes accessed | tf_op | source)
XLA Modules:
  0.0 68.4 jit_solution(12791408077728578860)
XLA Ops:
  0.0 0.0 copy-start.4
  0.0 0.0 copy-start.3
  0.0 0.8 %copy.7.forcing = f32[64,3]{1,0:T(8,128)S(1)} copy(f32[64,3]{0,1:T(4,128)} %param.11) | data formatting | bytes 1536 | tf_op args[5]
  0.8 0.0 copy-done.4
  0.8 0.0 copy-done.3
  0.8 0.0 copy-start
  0.8 1.0 %copy-done = f32[3,8,4096]{2,1,0:T(8,128)S(1)} copy-done((f32[3,8,4096]{2,1,0:T(8,128)S(1)}, f32[3,8,4096]{2,1,0:T(8,128)}, u32[]{:S(2)}) %copy-start) | copy-done | bytes 393240
  1.8 0.0 copy-start.1
  1.8 0.9 %copy-done.1 = bf16[3,16,16,128]{3,2,1,0:T(8,128)(2,1)S(1)} copy-done((bf16[3,16,16,128]{3,2,1,0:T(8,128)(2,1)S(1)}, bf16[3,16,16,128]{3,2,1,0:T(8,128)(2,1)}, u32[]{:S(2)}) %copy-start.1) | copy-done | bytes 196632
  2.7 0.0 copy-start.2
  2.7 0.9 %copy-done.2 = f32[16,16,128]{2,1,0:T(8,128)S(1)} copy-done((f32[16,16,128]{2,1,0:T(8,128)S(1)}, f32[16,16,128]{2,1,0:T(8,128)}, u32[]{:S(2)}) %copy-start.2) | copy-done | bytes 131096
  3.6 64.0 %shard_map.64 = f32[3,16,16,128]{3,2,1,0:T(8,128)S(1)} custom-call(s32[8]{0:T(128)S(1)} %copy-done.3, s32[1,1,8]{2,1,0:T(1,128)S(1)} %copy-done.4, f32[64,3]{1,0:T(8,128)S(1)} %copy.7.forcing, f32[3,8,4096]{2,1,0:T(8,128)S(1)} %copy-done, bf16[3,16,16,128]{3,2,1,0:T(8,128)(2,1)S(1)} %copy-done.1, f32[16,16,128]{2,1,0:T(8,128)S(1)} %copy-done.2), custom_call_target="tpu_custom_call" | custom-call | tf_op jit(solution)/shard_map/pallas_call | solution.py:388
  67.6 0.7 %copy.9 = f32[3,16,16,128]{3,2,1,0:T(8,128)} copy(f32[3,16,16,128]{3,2,1,0:T(8,128)S(1)} %shard_map.64) | data formatting | bytes 786432
Async XLA Ops:
  0.0 0.8 %copy-start.4 = (s32[1,1,8]{2,1,0:T(1,128)S(1)}, s32[1,1,8]{2,1,0:T(1,128)}, u32[]{:S(2)}) copy-start(s32[1,1,8]{2,1,0:T(1,128)} %fish.1) | copy-start | bytes 100
  0.0 0.8 %copy-start.3 = (s32[8]{0:T(128)S(1)}, s32[8]{0:T(128)}, u32[]{:S(2)}) copy-start(s32[8]{0:T(128)} %target.1) | copy-start | bytes 100
  0.8 1.0 %copy-start = (f32[3,8,4096]{2,1,0:T(8,128)S(1)}, f32[3,8,4096]{2,1,0:T(8,128)}, u32[]{:S(2)}) copy-start(f32[3,8,4096]{2,1,0:T(8,128)} %old.1) | copy-start | bytes 1179652
  1.8 0.9 %copy-start.1 = (bf16[3,16,16,128]{3,2,1,0:T(8,128)(2,1)S(1)}, bf16[3,16,16,128]{3,2,1,0:T(8,128)(2,1)}, u32[]{:S(2)}) copy-start(bf16[3,16,16,128]{3,2,1,0:T(8,128)(2,1)} %velocity.1) | copy-start | bytes 589828
  2.7 0.9 %copy-start.2 = (f32[16,16,128]{2,1,0:T(8,128)S(1)}, f32[16,16,128]{2,1,0:T(8,128)}, u32[]{:S(2)}) copy-start(f32[16,16,128]{2,1,0:T(8,128)} %chi.1) | copy-start | bytes 393220

commit v2 on v1

--- a/solution.py
+++ b/solution.py
@@ -16,7 +16,9 @@
 CHIPS = 4
 SLOTS = 8
 EDGE = 16
-TILES = 32
+PARTS = 6
+TILES = 16
+LAST = 7
 MESH = pl.DeviceIdType.MESH
 
 
@@ -28,17 +30,19 @@
     return lax.broadcasted_iota(jnp.int32, shape, len(shape) - 2)
 
 
-def swap_groups(tile):
-    row, group = rows_of(tile.shape), lanes_of(tile.shape) // EDGE
+def swap_groups(tiles):
+    row, group = rows_of((8, 128)), lanes_of((8, 128)) // EDGE
     for bit in (1, 2, 4):
         row_bit, group_bit = (row & bit) != 0, (group & bit) != 0
-        down = pltpu.roll(pltpu.roll(tile, bit, 0), 128 - EDGE * bit, 1)
-        if bit == 4:
+        same, moved = row_bit == group_bit, []
+        for tile in tiles:
+            down = pltpu.roll(pltpu.roll(tile, bit, 0), 128 - EDGE * bit, 1)
             up = down
-        else:
-            up = pltpu.roll(pltpu.roll(tile, 8 - bit, 0), EDGE * bit, 1)
-        tile = jnp.where(row_bit == group_bit, tile, jnp.where(row_bit, down, up))
-    return tile
+            if bit != 4:
+                up = pltpu.roll(pltpu.roll(tile, 8 - bit, 0), EDGE * bit, 1)
+            moved.append(jnp.where(same, tile, jnp.where(row_bit, down, up)))
+        tiles = moved
+    return tiles
 
 
 def pack_ends(tiles):
@@ -55,10 +59,10 @@
 
 
 def kernel(
-    target, fish, forcing, old, velocity, chi, out,
+    target, fish, forcing, old_far, velocity_far, chi_far, out, old, velocity, chi,
     gathered, meta, staged, outgoing, out_scales, incoming, in_scales, decoded,
     found, found_s, fields, face_y, halo_y, face_z, halo_z, slopes, weight, pull,
-    send_sems, recv_sems, local_sem,
+    send_sems, recv_sems, local_sems,
 ):
     stream, span, depth = (lax.axis_index(a) for a in ("stream", "span", "depth"))
     chip, core = stream // 2, stream % 2
@@ -82,6 +86,13 @@
         copies[key] = copy
         copy.start()
 
+    fetched = [
+        pltpu.make_async_copy(src, dst, local_sems.at[i])
+        for i, (src, dst) in enumerate(((old_far, old), (velocity_far, velocity), (chi_far, chi)))
+    ]
+    for copy in fetched:
+        copy.start()
+
     barrier = pltpu.get_barrier_semaphore()
     partners = [along("span", span, 1), along("span", span, -1)]
     partners += [along("depth", depth, 1), along("depth", depth, -1)]
@@ -89,45 +100,51 @@
     for partner in partners:
         pl.semaphore_signal(barrier, inc=1, device_id=partner, device_id_type=MESH)
 
-    for c in range(3):
-        top = jnp.abs(old[c, :, 0:128])
-        for t in range(1, TILES):
-            top = jnp.maximum(top, jnp.abs(old[c, :, 128 * t : 128 * t + 128]))
-        meta[0, c] = top * (1.0 / LEVELS)
-        inverse = LEVELS / jnp.maximum(top, 1e-30)
+    fetched[0].wait()
+    tops = [jnp.abs(old[c, :, 0:128]) for c in range(3)]
+    for t in range(1, 2 * TILES):
+        for c in range(3):
+            tops[c] = jnp.maximum(tops[c], jnp.abs(old[c, :, 128 * t : 128 * t + 128]))
+    top = jnp.maximum(jnp.maximum(tops[0], tops[1]), tops[2])
+    meta[0, 0] = top * (1.0 / LEVELS)
+    inverse = LEVELS / jnp.maximum(top, 1e-30)
+    for kind in range(PARTS):
+        c, first = kind // 2, kind % 2 * TILES
         for t in range(TILES):
-            staged[c][pl.ds(t, SLOTS, stride=TILES), :] = jnp.round(
-                old[c, :, 128 * t : 128 * t + 128] * inverse
-            )
+            begin = 128 * (first + t)
+            staged[kind][pl.ds(t, SLOTS, stride=TILES), :] = jnp.round(old[c, :, begin : begin + 128] * inverse)
         for b in range(SLOTS):
-            codes = staged[c][TILES * b : TILES * (b + 1), :]
-            gathered[c][b] = codes.astype(jnp.int32).astype(jnp.int16)
+            codes = staged[kind][TILES * b : TILES * (b + 1), :]
+            gathered[kind][b] = codes.astype(jnp.int32).astype(jnp.int16)
     label = jnp.zeros((8, 128), jnp.int32)
     for b in range(SLOTS):
         label = jnp.where(rows_of((8, 128)) == b, target[b], label)
-    meta[0, 3] = label.astype(jnp.float32)
+    meta[0, 1] = label.astype(jnp.float32)
 
     pl.semaphore_wait(barrier, len(partners))
 
-    def places(kind, e, part):
-        if kind == 3:
-            return meta.at[e]
-        if part is None:
-            return gathered[kind].at[pl.ds(8 * e, 8)]
-        return gathered[kind].at[pl.ds(8 * e + 4 * part, 4)]
+    def places(kind, place, count=8, skip=0):
+        if kind == PARTS:
+            return meta.at[pl.ds(place, count // 8)]
+        return gathered[kind].at[pl.ds(8 * place + skip, count)]
 
     def hop_right(kind, hop):
-        part = 0 if hop == 4 and kind < 3 else None
-        send(("r", kind, hop), places(kind, hop - 1, part), places(kind, hop, part), along("span", span, 1))
+        source = max(2 * hop - 3, 0)
+        count = 4 if hop == 4 and kind < PARTS else 8
+        send(("r", kind, hop), places(kind, source, count), places(kind, 2 * hop - 1, count), along("span", span, 1))
 
     def hop_left(kind, hop):
-        part = 1 if hop == 4 else None
-        send(("l", kind, hop), places(kind, (9 - hop) % 8, part), places(kind, 8 - hop, part), along("span", span, -1))
-
-    def to_core(kind, e, part=None):
-        send(("c", kind, e, part), places(kind, e, part), places(kind, 8 + e, part), other_core)
-
-    kinds = (3, 0, 1, 2)
+        source, to, count, skip = 2 * hop - 2, 2 * hop, 8, 0
+        if hop == 4:
+            to, count, skip = LAST, 4, 4
+        send(("l", kind, hop), places(kind, source, count, skip), places(kind, to, count, skip), along("span", span, -1))
+
+    def to_core(kind, hop):
+        first = max(2 * hop - 1, 0)
+        count = 8 if hop in (0, 4) else 16
+        send(("c", kind, hop), places(kind, first, count), places(kind, 8 + first, count), other_core)
+
+    kinds = (0, PARTS, *range(1, PARTS))
     for kind in kinds:
         hop_right(kind, 1)
         hop_left(kind, 1)
@@ -195,6 +212,7 @@
         z_after = jnp.where(lane == 127, end, pltpu.roll(here, 127, 1))
         return here, fields[n][i * 3 + c], fields[n][(i + 2) * 3 + c], y_before, y_after, z_before, z_after
 
+    fetched[1].wait()
     tiles = [[], [], []]
     for i in range(EDGE):
         for c in range(3):
@@ -209,19 +227,11 @@
         copies[("r", kind, hop)].wait_recv()
         if hop < 4:
             hop_right(kind, hop + 1)
-        if hop < 4 or kind == 3:
-            to_core(kind, hop)
-        else:
-            to_core(kind, hop, 0)
-        if hop == 4 and kind == 3:
-            return
-        copies[("l", kind, hop)].wait_recv()
-        if hop < 3 or kind < 3 and hop == 3:
+        if hop < 4 or kind < PARTS:
+            copies[("l", kind, hop)].wait_recv()
+        if hop < 3 or hop == 3 and kind < PARTS:
             hop_left(kind, hop + 1)
-        if hop < 4:
-            to_core(kind, 8 - hop)
-        else:
-            to_core(kind, 4, 1)
+        to_core(kind, hop)
 
     for kind in kinds:
         forward(kind, 1)
@@ -236,12 +246,13 @@
     for kind in kinds:
         forward(kind, 2)
 
+    fetched[2].wait()
     group = lanes_of(wide) // EDGE
     forces = []
     for c in range(3):
         force = jnp.zeros(wide, jnp.float32)
         for b in range(SLOTS):
-            force = jnp.where(group == b, forcing[fish[0, 0, b], c], force)
+            force = jnp.where(group == b, forcing[c, fish[0, 0, b]], force)
         forces.append(force)
     for i in range(EDGE):
         level = chi[i]
@@ -252,9 +263,9 @@
 
     for kind in kinds:
         forward(kind, 3)
-    forward(3, 4)
-    for e in range(8):
-        copies[("c", 3, e, None)].wait_recv()
+    forward(PARTS, 4)
+    for hop in range(5):
+        copies[("c", PARTS, hop)].wait_recv()
 
     shape = (8, 128)
     lane, row = lanes_of(shape), rows_of(shape)
@@ -262,9 +273,9 @@
     wanted = jnp.where(lane < CHIPS * SLOTS, owner * SLOTS + lane % 8, -1).astype(jnp.float32)
     at = jnp.zeros(shape, jnp.float32)
     for e in range(16):
-        at = at + jnp.where(meta[e, 3] == wanted, (row + (8 * e + 1)).astype(jnp.float32), 0.0)
+        at = at + jnp.where(meta[e, 1] == wanted, (row + (8 * e + 1)).astype(jnp.float32), 0.0)
     found[...] = jnp.broadcast_to(jnp.sum(at, axis=0, keepdims=True), shape).astype(jnp.int32)
-    copy = pltpu.make_async_copy(found, found_s, local_sem)
+    copy = pltpu.make_async_copy(found, found_s, local_sems.at[3])
     copy.start()
     copy.wait()
     where_from = []
@@ -273,21 +284,17 @@
         code = found_s[0, q]
         block = jnp.minimum(jnp.maximum(code - 1, 0), 127)
         where_from.append(block)
-        valid = jnp.where(code > 0, 1.0, 0.0)
-        for c in range(3):
-            scale = meta[block // 8, c, pl.ds(block % 8, 1), :] * valid
-            if k == 0:
-                in_scales[0, c, j : j + 1, :] = scale
-            else:
-                out_scales[k - 1, c, j : j + 1, :] = scale
+        scale = meta[block >> 3, 0, pl.ds(block & 7, 1), :] * jnp.where(code > 0, 1.0, 0.0)
+        if k == 0:
+            in_scales[0, j : j + 1, :] = scale
+        else:
+            out_scales[k - 1, j : j + 1, :] = scale
     for k in (2, 1, 3):
         send(("s", k), out_scales.at[k - 1], in_scales.at[k], along("stream", stream, 2 * k))
 
-    for kind in (0, 1, 2):
-        forward(kind, 4)
-        for e in range(8):
-            for part in (0, 1) if e == 4 else (None,):
-                copies[("c", kind, e, part)].wait_recv()
+    def pick(kind):
+        for hop in range(5):
+            copies[("c", kind, hop)].wait_recv()
         for k in (2, 1, 3, 0):
             for j in range(SLOTS):
                 block = gathered[kind][where_from[k * SLOTS + j]]
@@ -298,24 +305,30 @@
             if k:
                 send(("x", kind, k), outgoing[kind].at[k - 1], incoming[kind].at[k], along("stream", stream, 2 * k))
 
+    for kind in range(PARTS):
+        forward(kind, 4)
+        if kind:
+            pick(kind - 1)
+    pick(PARTS - 1)
+
     for k in (2, 1, 3):
         copies[("s", k)].wait_recv()
     tiles = [[], [], []]
-    for c in range(3):
+    for kind in range(PARTS):
+        c, first = kind // 2, kind % 2 * (EDGE // 2)
         for k in (2, 1, 3):
-            copies[("x", c, k)].wait_recv()
+            copies[("x", kind, k)].wait_recv()
         for j in range(SLOTS):
-            total = incoming[c][0, j].astype(jnp.float32) * in_scales[0, c, j : j + 1, :]
+            total = incoming[kind][0, j].astype(jnp.float32) * in_scales[0, j : j + 1, :]
             for k in range(1, CHIPS):
-                total = total + incoming[c][k, j].astype(jnp.float32) * in_scales[k, c, j : j + 1, :]
-            decoded[c][TILES * j : TILES * (j + 1), :] = total
-        for i in range(EDGE):
-            halves = [swap_groups(decoded[c][pl.ds(2 * i + h, SLOTS, stride=TILES), :]) for h in (0, 1)]
-            for h in (0, 1):
-                fields[0][(i + 1) * 3 + c, 8 * h : 8 * h + 8, :] = halves[h]
-            face_y[0][0, i * 3 + c : i * 3 + c + 1, :] = halves[0][0:1]
-            face_y[0][1, i * 3 + c : i * 3 + c + 1, :] = halves[1][7:8]
-            tiles[c] += halves
+                total = total + incoming[kind][k, j].astype(jnp.float32) * in_scales[k, j : j + 1, :]
+            decoded[kind][TILES * j : TILES * (j + 1), :] = total
+        moved = swap_groups([decoded[kind][pl.ds(t, SLOTS, stride=TILES), :] for t in range(TILES)])
+        tiles[c] += moved
+        for t, tile in enumerate(moved):
+            i, h = first + t // 2, t % 2
+            fields[0][(i + 1) * 3 + c, 8 * h : 8 * h + 8, :] = tile
+            face_y[0][h, i * 3 + c : i * 3 + c + 1, :] = tile[7 * h : 7 * h + 1]
     keep_ends(0, tiles)
 
     for section in range(SECTIONS):
@@ -361,14 +374,17 @@
     f32, i16 = jnp.float32, jnp.int16
     v = pltpu.VMEM
     scratch = [
-        [v((128, TILES, 128), i16)] * 3,
-        v((16, 4, 8, 128), f32),
-        [v((SLOTS * TILES, 128), f32)] * 3,
-        [v((CHIPS - 1, SLOTS, TILES, 128), i16)] * 3,
-        v((CHIPS - 1, 3, SLOTS, 128), f32),
-        [v((CHIPS, SLOTS, TILES, 128), i16)] * 3,
-        v((CHIPS, 3, SLOTS, 128), f32),
-        [v((SLOTS * TILES, 128), f32)] * 3,
+        v((3, SLOTS, 2 * TILES * 128), f32),
+        v(velocity.shape, velocity.dtype),
+        v(chi.shape, f32),
+        [v((128, TILES, 128), i16)] * PARTS,
+        v((16, 2, 8, 128), f32),
+        [v((SLOTS * TILES, 128), f32)] * PARTS,
+        [v((CHIPS - 1, SLOTS, TILES, 128), i16)] * PARTS,
+        v((CHIPS - 1, SLOTS, 128), f32),
+        [v((CHIPS, SLOTS, TILES, 128), i16)] * PARTS,
+        v((CHIPS, SLOTS, 128), f32),
+        [v((SLOTS * TILES, 128), f32)] * PARTS,
         v((8, 128), jnp.int32),
         pltpu.SMEM((8, 128), jnp.int32),
         [v((18 * 3, EDGE, 128), f32)] * 5,
@@ -379,22 +395,23 @@
         v((9 * EDGE, EDGE, 128), f32),
         v((EDGE, EDGE, 128), f32),
         v((3 * EDGE, EDGE, 128), f32),
-        pltpu.SemaphoreType.DMA((128,)),
-        pltpu.SemaphoreType.DMA((128,)),
-        pltpu.SemaphoreType.DMA,
+        pltpu.SemaphoreType.DMA((192,)),
+        pltpu.SemaphoreType.DMA((192,)),
+        pltpu.SemaphoreType.DMA((4,)),
     ]
     smem = pl.BlockSpec(memory_space=pltpu.SMEM)
+    far = pl.BlockSpec(memory_space=pl.ANY)
     vmem = pl.BlockSpec(memory_space=pltpu.VMEM)
     return pl.pallas_call(
         kernel,
         out_shape=jax.ShapeDtypeStruct(velocity.shape, f32),
-        in_specs=[smem, smem, smem, vmem, vmem, vmem],
+        in_specs=[smem, smem, smem, far, far, far],
         out_specs=vmem,
         scratch_shapes=scratch,
         compiler_params=pltpu.CompilerParams(
-            collective_id=0, has_side_effects=True, vmem_limit_bytes=40 * 1024 * 1024
+            collective_id=0, has_side_effects=True, vmem_limit_bytes=63 * 1024 * 1024
         ),
-    )(target, fish, fish_forcing, old_adjoint, velocity, chi)
+    )(target, fish, fish_forcing.T, old_adjoint, velocity, chi)
 
 
 def solution(mesh):

time: 68.6 us -> 66.7 us (0.972)
  local copies, waits for them, and re-layouts: 4.37 us -> 1.77 us
  Pallas kernels: 64 us -> 64.7 us
    unnamed x12 -> x1, local copies, waits for them, and re-layouts: 4.37 us -> 1.77 us
    pallas_call x1, Pallas kernels: 64 us -> 64.7 us  [body(): pl.pallas_call(kernel, out_shape=jax.ShapeDtypeStruct(velocity.shape, f32...]
where the time goes in v2:
time: 66.7 us; the launch traced here: 66.5 us
  Pallas kernels  64.7 us (97%)
  local copies, waits for them, and re-layouts  1.77 us (3%)
    pallas_call x1, Pallas kernels, body(): pl.pallas_call(kernel, out_shape=jax.ShapeDtypeStruct(velocity.shape, f32...  64.7 us
    unnamed x1, local copies, waits for them, and re-layouts  1.77 us

profile of v2, /device:TPU:1, one launch (start us, length us, event | category | flops | bytes accessed | tf_op | source)
XLA Modules:
  0.0 66.5 jit_solution(13108114645366534283)
XLA Ops:
  0.0 64.7 %shard_map.64 = f32[3,16,16,128]{3,2,1,0:T(8,128)} custom-call(s32[8]{0:T(128)} %target.1, s32[1,1,8]{2,1,0:T(1,128)} %fish.1, f32[3,64]{1,0:T(4,128)} %bitcast.1, f32[3,8,4096]{2,1,0:T(8,128)} %old_far.1, bf16[3,16,16,128]{3,2,1,0:T(8,128)(2,1)} %velocity_far.1, f32[16,16,128]{2,1,0:T(8,128)} %chi_far.1), custom_call_target="tpu_custom_call" | custom-call | tf_op jit(solution)/shard_map/pallas_call | solution.py:405
  64.7 1.8 %copy.8 = f32[3,16,16,128]{3,2,1,0:T(8,128)} copy(f32[3,16,16,128]{3,2,1,0:T(8,128)} %shard_map.64) | data formatting | bytes 786432

commit v3 on v2

--- a/solution.py
+++ b/solution.py
@@ -46,22 +46,34 @@
 
 
 def pack_ends(tiles):
-    pair = ((lanes_of((8, 128)) + 1) & 127) // 2
+    place = ((lanes_of((8, 128)) + 2) & 127) // 4
     shift = 1
     while len(tiles) > 1:
-        later = (pair & shift) != 0
+        later = (place & shift) != 0
         tiles = [
-            jnp.where(later, pltpu.roll(b, 2 * shift, 1), a)
+            jnp.where(later, pltpu.roll(b, 4 * shift, 1), a)
             for a, b in zip(tiles[0::2], tiles[1::2])
         ]
         shift *= 2
     return tiles[0]
 
 
+def advected(here, near, carried, slope):
+    values = []
+    for c in range(3):
+        value = here[c]
+        for k in range(3):
+            value = value + carried[k] * (near[c][2 * k + 1] - near[c][2 * k])
+            value = value - here[k] * slope(c, k)
+        values.append(value)
+    return values
+
+
 def kernel(
     target, fish, forcing, old_far, velocity_far, chi_far, out, old, velocity, chi,
     gathered, meta, staged, outgoing, out_scales, incoming, in_scales, decoded,
-    found, found_s, fields, face_y, halo_y, face_z, halo_z, slopes, weight, pull,
+    found, found_s, fields, face_y, halo_y, face_z, halo_z, corners, corners_in, edge_z,
+    moved_x, moved_y, moved_z, slopes, slopes_y, slopes_z, carried_z, weight, pull,
     send_sems, recv_sems, local_sems,
 ):
     stream, span, depth = (lax.axis_index(a) for a in ("stream", "span", "depth"))
@@ -97,6 +109,14 @@
     partners = [along("span", span, 1), along("span", span, -1)]
     partners += [along("depth", depth, 1), along("depth", depth, -1)]
     partners += [along("stream", stream, s) for s in (1, -1, 2, 4, 6)]
+    sides = (-1, 1)
+    beside = {"stream": stream, "span": span, "depth": depth}
+
+    def diagonal(axis, step, other, other_step):
+        return {**along(axis, beside[axis], step), **along(other, beside[other], other_step)}
+
+    pairs = (("stream", "span"), ("stream", "depth"), ("span", "depth"))
+    partners += [diagonal(a, i, b, j) for a, b in pairs for i in sides for j in sides]
     for partner in partners:
         pl.semaphore_signal(barrier, inc=1, device_id=partner, device_id_type=MESH)
 
@@ -144,84 +164,163 @@
         count = 8 if hop in (0, 4) else 16
         send(("c", kind, hop), places(kind, first, count), places(kind, 8 + first, count), other_core)
 
-    kinds = (0, PARTS, *range(1, PARTS))
+    kinds = (PARTS, *range(PARTS))
     for kind in kinds:
         hop_right(kind, 1)
         hop_left(kind, 1)
     for kind in kinds:
         to_core(kind, 0)
 
+    wide, small = (EDGE, 128), (8, 128)
+    lane, row, lane8, row8 = lanes_of(wide), rows_of(wide), lanes_of(small), rows_of(small)
+    place8 = ((lane8 + 1) & 127) // 4
+    after8 = (lane8 & 3) == 3
+    odd8 = (place8 & 1) == 1
+
+    def keep_row(n, i, c, y, layer, value):
+        face_y[n][y][layer * 3 + c, i : i + 1, :] = value
+        if layer == 0 and i in (0, EDGE - 1):
+            corners[n][(i > 0) * 2 + y, c : c + 1, :] = value
+
     def keep_faces(n, i, c, value):
-        face_y[n][0, i * 3 + c : i * 3 + c + 1, :] = value[0:1]
-        face_y[n][1, i * 3 + c : i * 3 + c + 1, :] = value[EDGE - 1 : EDGE]
-
-    def keep_ends(n, tiles):
+        for layer in (0, 1):
+            keep_row(n, i, c, 0, layer, value[layer : layer + 1])
+            keep_row(n, i, c, 1, layer, value[EDGE - 1 - layer : EDGE - layer])
+
+    def start_halo(n, tiles):
+        field = fields[n]
+        for y in (1, 0):
+            send((n, "y", y), face_y[n][y], halo_y[n].at[1 - y], along("span", span, sides[y]))
         for c in range(3):
             face_z[n][c] = pack_ends(tiles[c])
-
-    def start_halo(n):
-        field = fields[n]
-        send((n, "x", 0), field.at[pl.ds(48, 3)], field.at[pl.ds(0, 3)], along("stream", stream, 1))
-        send((n, "x", 1), field.at[pl.ds(3, 3)], field.at[pl.ds(51, 3)], along("stream", stream, -1))
-        send((n, "y", 0), face_y[n].at[1], halo_y[n].at[0], along("span", span, 1))
-        send((n, "y", 1), face_y[n].at[0], halo_y[n].at[1], along("span", span, -1))
-        send((n, "z", 0), face_z[n], halo_z[n].at[0], along("depth", depth, 1))
-        send((n, "z", 1), face_z[n], halo_z[n].at[1], along("depth", depth, -1))
-
-    def finish_halo(n):
+        for z in (0, 1):
+            send((n, "z", z), face_z[n], halo_z[n].at[1 - z], along("depth", depth, sides[z]))
+        send((n, "x", 1), field.at[pl.ds(48, 6)], field.at[pl.ds(0, 6)], along("stream", stream, 1))
+        send((n, "x", 0), field.at[pl.ds(6, 6)], field.at[pl.ds(54, 6)], along("stream", stream, -1))
+        for x in (0, 1):
+            for y in (0, 1):
+                send(
+                    (n, "xy", x, y),
+                    corners[n].at[2 * x + y],
+                    corners_in[n].at[3 - 2 * x - y],
+                    diagonal("stream", sides[x], "span", sides[y]),
+                )
+        for number, axis in enumerate(("stream", "span")):
+            for i in (0, 1):
+                for z in (0, 1):
+                    send(
+                        (n, axis, i, z),
+                        face_z[n],
+                        edge_z[n].at[4 * number + 3 - 2 * i - z],
+                        diagonal(axis, sides[i], "depth", sides[z]),
+                    )
+
+    def ends(before, after, c, layer=1):
+        low = jnp.where(depth == 0, 0.0, pltpu.roll(before[c], layer, 1))
+        high = jnp.where(depth == RING - 1, 0.0, pltpu.roll(after[c], 128 - layer, 1))
+        return jnp.where(after8, high, low)
+
+    def finish_faces(n):
         for axis in ("x", "y", "z"):
             for side in (0, 1):
                 copies[(n, axis, side)].wait_recv()
-
-        @pl.when(stream == 0)
-        def _():
-            fields[n][0:3] = jnp.zeros((3, EDGE, 128), jnp.float32)
-
-        @pl.when(stream == RING - 1)
-        def _():
-            fields[n][51:54] = jnp.zeros((3, EDGE, 128), jnp.float32)
-
-        @pl.when(span == 0)
-        def _():
-            halo_y[n][0] = jnp.zeros((48, 128), jnp.float32)
-
-        @pl.when(span == RING - 1)
-        def _():
-            halo_y[n][1] = jnp.zeros((48, 128), jnp.float32)
-
-        ends = []
-        odd = (lanes_of((8, 128)) & 1) == 1
-        for c in range(3):
-            before = jnp.where(depth == 0, 0.0, pltpu.roll(halo_z[n][0, c], 1, 1))
-            after = jnp.where(depth == RING - 1, 0.0, pltpu.roll(halo_z[n][1, c], 127, 1))
-            ends.append(jnp.where(odd, after, before))
-        return ends
-
-    wide = (EDGE, 128)
-
-    def around(n, ends, i, c):
-        here = fields[n][(i + 1) * 3 + c]
-        row, lane = rows_of(wide), lanes_of(wide)
-        at = i * 3 + c
-        y_before = jnp.where(row == 0, halo_y[n][0, at : at + 1, :], pltpu.roll(here, 1, 0))
-        y_after = jnp.where(row == EDGE - 1, halo_y[n][1, at : at + 1, :], pltpu.roll(here, EDGE - 1, 0))
+        for end, x in ((0, 0), (RING - 1, 1)):
+
+            @pl.when(stream == end)
+            def _():
+                fields[n][54 * x : 54 * x + 6] = jnp.zeros((6, EDGE, 128), jnp.float32)
+
+            @pl.when(span == end)
+            def _():
+                halo_y[n][x] = jnp.zeros((6, EDGE, 128), jnp.float32)
+
+        return [ends(halo_z[n].at[0], halo_z[n].at[1], c) for c in range(3)]
+
+    def finish_diagonals(n):
+        for key in [key for key in copies if key[0] == n and key[1] in ("xy", "stream", "span")]:
+            copies[key].wait_recv()
+        for end, x in ((0, 0), (RING - 1, 1)):
+
+            @pl.when(stream == end)
+            def _():
+                for y in (0, 1):
+                    corners_in[n][2 * x + y] = jnp.zeros(small, jnp.float32)
+
+            @pl.when(span == end)
+            def _():
+                for y in (0, 1):
+                    corners_in[n][2 * y + x] = jnp.zeros(small, jnp.float32)
+
+        second = [ends(halo_z[n].at[0], halo_z[n].at[1], c, 2) for c in range(3)]
+        outside = (stream == 0, stream == RING - 1, span == 0, span == RING - 1)
+        edges = [
+            [
+                jnp.where(outside[e], 0.0, ends(edge_z[n].at[2 * e], edge_z[n].at[2 * e + 1], c))
+                for c in range(3)
+            ]
+            for e in range(4)
+        ]
+        return second, edges
+
+    def around(planes, low, high, ends, first):
+        before, here, after = planes
+        y_before = jnp.where(row == 0, low, pltpu.roll(here, 1, 0))
+        y_after = jnp.where(row == EDGE - 1, high, pltpu.roll(here, EDGE - 1, 0))
         end = jnp.concatenate(
-            [pltpu.roll(ends[c], (128 - 2 * v) % 128, 1) for v in (2 * i, 2 * i + 1)], axis=0
+            [pltpu.roll(ends, (128 - 4 * v) % 128, 1) for v in (first, first + 1)], axis=0
         )
         z_before = jnp.where(lane == 0, end, pltpu.roll(here, 1, 1))
         z_after = jnp.where(lane == 127, end, pltpu.roll(here, 127, 1))
-        return here, fields[n][i * 3 + c], fields[n][(i + 2) * 3 + c], y_before, y_after, z_before, z_after
+        return before, after, y_before, y_after, z_before, z_after
+
+    def plane_near(n, halo, i, c):
+        beyond, _, edges = halo
+        planes = [fields[n][(i + 1 + d) * 3 + c] for d in range(3)]
+        if i < 0:
+            low, high = (corners_in[n][y, c : c + 1, :] for y in (0, 1))
+            return around(planes, low, high, edges[0][c], 30)
+        if i == EDGE:
+            low, high = (corners_in[n][2 + y, c : c + 1, :] for y in (0, 1))
+            return around(planes, low, high, edges[1][c], 0)
+        low, high = (halo_y[n][y, c, i : i + 1, :] for y in (0, 1))
+        return around(planes, low, high, beyond[c], 2 * i)
+
+    def row_near(n, halo, y, c):
+        here, outer, inner = halo_y[n][y, c], halo_y[n][y, 3 + c], face_y[n][y][c]
+        x_before = jnp.where(row == 0, corners_in[n][y, c : c + 1, :], pltpu.roll(here, 1, 0))
+        x_after = jnp.where(row == EDGE - 1, corners_in[n][2 + y, c : c + 1, :], pltpu.roll(here, EDGE - 1, 0))
+        edge = halo[2][2 + y][c][7 - 7 * y : 8 - 7 * y, :]
+        columns = [
+            jnp.sum(jnp.where(lane == ((8 * row + 4 - 4 * y - z) & 127), edge, 0.0), axis=1, keepdims=True)
+            for z in (0, 1)
+        ]
+        z_before = jnp.where(lane == 0, columns[0], pltpu.roll(here, 1, 1))
+        z_after = jnp.where(lane == 127, columns[1], pltpu.roll(here, 127, 1))
+        y_pair = (inner, outer) if y else (outer, inner)
+        return x_before, x_after, *y_pair, z_before, z_after
+
+    def end_near(n, halo, c):
+        here, outer, inner = halo[0][c], halo[1][c], face_z[n][c]
+        x_low, x_high, y_low, y_high = (edge[c] for edge in halo[2])
+        x_before = jnp.where(place8 < 2, pltpu.roll(x_low, 8, 1), pltpu.roll(here, 8, 1))
+        x_after = jnp.where(place8 >= 30, pltpu.roll(x_high, 120, 1), pltpu.roll(here, 120, 1))
+        into = jnp.where(odd8, pltpu.roll(here, 4, 1), pltpu.roll(y_low, 124, 1))
+        y_before = jnp.where(row8 == 0, pltpu.roll(into, 1, 0), pltpu.roll(here, 1, 0))
+        into = jnp.where(odd8, pltpu.roll(y_high, 4, 1), pltpu.roll(here, 124, 1))
+        y_after = jnp.where(row8 == 7, pltpu.roll(into, 7, 0), pltpu.roll(here, 7, 0))
+        z_before = jnp.where(after8, inner, outer)
+        z_after = jnp.where(after8, outer, inner)
+        return x_before, x_after, y_before, y_after, z_before, z_after
 
     fetched[1].wait()
     tiles = [[], [], []]
     for i in range(EDGE):
         for c in range(3):
             value = velocity[c, i].astype(jnp.float32)
-            fields[4][(i + 1) * 3 + c] = value
-            keep_faces(4, i, c, value)
+            fields[2][(i + 2) * 3 + c] = value
+            keep_faces(2, i, c, value)
             tiles[c] += [value[0:8], value[8:16]]
-    keep_ends(4, tiles)
-    start_halo(4)
+    start_halo(2, tiles)
 
     def forward(kind, hop):
         copies[("r", kind, hop)].wait_recv()
@@ -236,45 +335,22 @@
     for kind in kinds:
         forward(kind, 1)
 
-    ends = finish_halo(4)
-    for i in range(EDGE):
-        for k in range(3):
-            _, *near = around(4, ends, i, k)
-            for axis in range(3):
-                slopes[(axis * 3 + k) * EDGE + i] = ADVECT * (near[2 * axis + 1] - near[2 * axis])
-
     for kind in kinds:
         forward(kind, 2)
 
-    fetched[2].wait()
-    group = lanes_of(wide) // EDGE
-    forces = []
-    for c in range(3):
-        force = jnp.zeros(wide, jnp.float32)
-        for b in range(SLOTS):
-            force = jnp.where(group == b, forcing[c, fish[0, 0, b]], force)
-        forces.append(force)
-    for i in range(EDGE):
-        level = chi[i]
-        share = 1.0 / (1.0 + level)
-        weight[i] = share
-        for c in range(3):
-            pull[i * 3 + c] = level * share * forces[c]
-
     for kind in kinds:
         forward(kind, 3)
-    forward(PARTS, 4)
+    for kind in (PARTS, 0, 1, 2):
+        forward(kind, 4)
     for hop in range(5):
         copies[("c", PARTS, hop)].wait_recv()
 
-    shape = (8, 128)
-    lane, row = lanes_of(shape), rows_of(shape)
-    owner = (2 * ((chip + lane // 8) % CHIPS) + core) * RING + span
-    wanted = jnp.where(lane < CHIPS * SLOTS, owner * SLOTS + lane % 8, -1).astype(jnp.float32)
-    at = jnp.zeros(shape, jnp.float32)
+    owner = (2 * ((chip + lane8 // 8) % CHIPS) + core) * RING + span
+    wanted = jnp.where(lane8 < CHIPS * SLOTS, owner * SLOTS + lane8 % 8, -1).astype(jnp.float32)
+    at = jnp.zeros(small, jnp.float32)
     for e in range(16):
-        at = at + jnp.where(meta[e, 1] == wanted, (row + (8 * e + 1)).astype(jnp.float32), 0.0)
-    found[...] = jnp.broadcast_to(jnp.sum(at, axis=0, keepdims=True), shape).astype(jnp.int32)
+        at = at + jnp.where(meta[e, 1] == wanted, (row8 + (8 * e + 1)).astype(jnp.float32), 0.0)
+    found[...] = jnp.broadcast_to(jnp.sum(at, axis=0, keepdims=True), small).astype(jnp.int32)
     copy = pltpu.make_async_copy(found, found_s, local_sems.at[3])
     copy.start()
     copy.wait()
@@ -306,10 +382,41 @@
                 send(("x", kind, k), outgoing[kind].at[k - 1], incoming[kind].at[k], along("stream", stream, 2 * k))
 
     for kind in range(PARTS):
-        forward(kind, 4)
-        if kind:
-            pick(kind - 1)
-    pick(PARTS - 1)
+        pick(kind)
+        if kind + 3 < PARTS:
+            forward(kind + 3, 4)
+
+    fetched[2].wait()
+    group = lane // EDGE
+    forces = []
+    for c in range(3):
+        force = jnp.zeros(wide, jnp.float32)
+        for b in range(SLOTS):
+            force = jnp.where(group == b, forcing[c, fish[0, 0, b]], force)
+        forces.append(force)
+    for i in range(EDGE):
+        level = chi[i]
+        share = 1.0 / (1.0 + level)
+        weight[i] = share
+        for c in range(3):
+            pull[i * 3 + c] = level * share * forces[c]
+
+    beyond = finish_faces(2)
+    halo = (beyond, *finish_diagonals(2))
+    for k in range(3):
+        carried_z[k] = ADVECT * halo[0][k]
+        beside_ends = end_near(2, halo, k)
+        beside_rows = [row_near(2, halo, y, k) for y in (0, 1)]
+        for axis in range(3):
+            slopes_z[axis * 3 + k] = ADVECT * (beside_ends[2 * axis + 1] - beside_ends[2 * axis])
+            for y in (0, 1):
+                slopes_y[y * 9 + axis * 3 + k] = ADVECT * (beside_rows[y][2 * axis + 1] - beside_rows[y][2 * axis])
+    for i in range(-1, EDGE + 1):
+        for k in range(3):
+            near = plane_near(2, halo, i, k)
+            for axis in range(3):
+                slopes[(axis * 3 + k) * 18 + i + 1] = ADVECT * (near[2 * axis + 1] - near[2 * axis])
+
 
     for k in (2, 1, 3):
         copies[("s", k)].wait_recv()
@@ -327,44 +434,54 @@
         tiles[c] += moved
         for t, tile in enumerate(moved):
             i, h = first + t // 2, t % 2
-            fields[0][(i + 1) * 3 + c, 8 * h : 8 * h + 8, :] = tile
-            face_y[0][h, i * 3 + c : i * 3 + c + 1, :] = tile[7 * h : 7 * h + 1]
-    keep_ends(0, tiles)
+            fields[0][(i + 2) * 3 + c, 8 * h : 8 * h + 8, :] = tile
+            for layer in (0, 1):
+                at = 7 - layer if h else layer
+                keep_row(0, i, c, h, layer, tile[at : at + 1])
 
     for section in range(SECTIONS):
-        n = 2 * section
-        start_halo(n)
-        ends = finish_halo(n)
-        tiles = [[], [], []]
-        for i in range(EDGE):
-            near = [around(n, ends, i, c) for c in range(3)]
-            carried = [ADVECT * fields[4][(i + 1) * 3 + k] for k in range(3)]
+        start_halo(section, tiles)
+        beyond = finish_faces(section)
+        halo = (beyond, None, None)
+        for i in (*range(EDGE), -1, EDGE):
+            if i < 0:
+                halo = (beyond, *finish_diagonals(section))
+            here = [fields[section][(i + 2) * 3 + c] for c in range(3)]
+            near = [plane_near(section, halo, i, c) for c in range(3)]
+            carried = [ADVECT * fields[2][(i + 2) * 3 + k] for k in range(3)]
+            values = advected(here, near, carried, lambda c, k: slopes[(c * 3 + k) * 18 + i + 1])
             for c in range(3):
-                value = near[c][0]
-                for k in range(3):
-                    value = value + carried[k] * (near[c][2 * k + 2] - near[c][2 * k + 1])
-                    value = value - near[k][0] * slopes[(c * 3 + k) * EDGE + i]
-                fields[n + 1][(i + 1) * 3 + c] = value
-                keep_faces(n + 1, i, c, value)
-                tiles[c] += [value[0:8], value[8:16]]
-        keep_ends(n + 1, tiles)
-        start_halo(n + 1)
-        ends = finish_halo(n + 1)
+                value = values[c]
+                if i in (-1, EDGE):
+                    value = jnp.where(stream == (0 if i < 0 else RING - 1), 0.0, value)
+                moved_x[(i + 1) * 3 + c] = value
+        here = beyond
+        near = [end_near(section, halo, c) for c in range(3)]
+        values = advected(here, near, [carried_z[k] for k in range(3)], lambda c, k: slopes_z[c * 3 + k])
+        for c in range(3):
+            moved_z[c] = jnp.where(jnp.where(after8, RING - 1, 0) == depth, 0.0, values[c])
+        for y in (0, 1):
+            here = [halo_y[section][y, c] for c in range(3)]
+            near = [row_near(section, halo, y, c) for c in range(3)]
+            carried = [ADVECT * halo_y[2][y, k] for k in range(3)]
+            values = advected(here, near, carried, lambda c, k: slopes_y[y * 9 + c * 3 + k])
+            for c in range(3):
+                moved_y[y * 3 + c] = jnp.where(span == (RING - 1) * y, 0.0, values[c])
         tiles = [[], [], []]
         for i in range(EDGE):
             share = weight[i]
             for c in range(3):
-                here, *near = around(n + 1, ends, i, c)
+                planes = [moved_x[(i + d) * 3 + c] for d in range(3)]
+                low, high = (moved_y[y * 3 + c, i : i + 1, :] for y in (0, 1))
+                near = around(planes, low, high, moved_z[c], 2 * i)
                 total = (near[0] + near[1]) + (near[2] + near[3]) + (near[4] + near[5])
-                value = (here + DIFFUSE * (total - 6.0 * here)) * share + pull[i * 3 + c]
+                value = (planes[1] + DIFFUSE * (total - 6.0 * planes[1])) * share + pull[i * 3 + c]
                 if section == SECTIONS - 1:
                     out[c, i] = value
                 else:
-                    fields[n + 2][(i + 1) * 3 + c] = value
-                    keep_faces(n + 2, i, c, value)
+                    fields[section + 1][(i + 2) * 3 + c] = value
+                    keep_faces(section + 1, i, c, value)
                     tiles[c] += [value[0:8], value[8:16]]
-        if section < SECTIONS - 1:
-            keep_ends(n + 2, tiles)
 
     for copy in copies.values():
         copy.wait_send()
@@ -387,12 +504,21 @@
         [v((SLOTS * TILES, 128), f32)] * PARTS,
         v((8, 128), jnp.int32),
         pltpu.SMEM((8, 128), jnp.int32),
-        [v((18 * 3, EDGE, 128), f32)] * 5,
-        [v((2, 48, 128), f32)] * 5,
-        [v((2, 48, 128), f32)] * 5,
-        [v((3, 8, 128), f32)] * 5,
-        [v((2, 3, 8, 128), f32)] * 5,
-        v((9 * EDGE, EDGE, 128), f32),
+        [v((20 * 3, EDGE, 128), f32)] * 3,
+        [[v((6, EDGE, 128), f32)] * 2] * 3,
+        [v((2, 6, EDGE, 128), f32)] * 3,
+        [v((3, 8, 128), f32)] * 3,
+        [v((2, 3, 8, 128), f32)] * 3,
+        [v((4, 8, 128), f32)] * 3,
+        [v((4, 8, 128), f32)] * 3,
+        [v((8, 3, 8, 128), f32)] * 3,
+        v((18 * 3, EDGE, 128), f32),
+        v((6, EDGE, 128), f32),
+        v((3, 8, 128), f32),
+        v((9 * 18, EDGE, 128), f32),
+        v((18, EDGE, 128), f32),
+        v((9, 8, 128), f32),
+        v((3, 8, 128), f32),
         v((EDGE, EDGE, 128), f32),
         v((3 * EDGE, EDGE, 128), f32),
         pltpu.SemaphoreType.DMA((192,)),

time: 66.7 us -> 63.4 us (0.951)
  Pallas kernels: 64.7 us -> 61.5 us
    pallas_call x1, Pallas kernels: 64.7 us -> 61.5 us  [body(): pl.pallas_call(kernel, out_shape=jax.ShapeDtypeStruct(velocity.shape, f32...]
where the time goes in v3:
time: 63.4 us; the launch traced here: 63.2 us
  Pallas kernels  61.5 us (97%)
  local copies, waits for them, and re-layouts  1.77 us (3%)
    pallas_call x1, Pallas kernels, body(): pl.pallas_call(kernel, out_shape=jax.ShapeDtypeStruct(velocity.shape, f32...  61.5 us
    unnamed x1, local copies, waits for them, and re-layouts  1.77 us

profile of v3, /device:TPU:1, one launch (start us, length us, event | category | flops | bytes accessed | tf_op | source)
XLA Modules:
  0.0 63.2 jit_solution(5428320112203842321)
XLA Ops:
  0.0 61.5 %shard_map.64 = f32[3,16,16,128]{3,2,1,0:T(8,128)} custom-call(s32[8]{0:T(128)} %target.1, s32[1,1,8]{2,1,0:T(1,128)} %fish.1, f32[3,64]{1,0:T(4,128)} %bitcast.1, f32[3,8,4096]{2,1,0:T(8,128)} %old_far.1, bf16[3,16,16,128]{3,2,1,0:T(8,128)(2,1)} %velocity_far.1, f32[16,16,128]{2,1,0:T(8,128)} %chi_far.1), custom_call_target="tpu_custom_call" | custom-call | tf_op jit(solution)/shard_map/pallas_call | solution.py:531
  61.5 1.8 %copy.8 = f32[3,16,16,128]{3,2,1,0:T(8,128)} copy(f32[3,16,16,128]{3,2,1,0:T(8,128)} %shard_map.64) | data formatting | bytes 786432

commit v4 on v3

--- a/solution.py
+++ b/solution.py
@@ -16,8 +16,9 @@
 CHIPS = 4
 SLOTS = 8
 EDGE = 16
-PARTS = 6
-TILES = 16
+PARTS = 3
+EACH = PARTS // 3
+TILES = 32 // EACH
 LAST = 7
 MESH = pl.DeviceIdType.MESH
 
@@ -115,21 +116,19 @@
     def diagonal(axis, step, other, other_step):
         return {**along(axis, beside[axis], step), **along(other, beside[other], other_step)}
 
-    pairs = (("stream", "span"), ("stream", "depth"), ("span", "depth"))
-    partners += [diagonal(a, i, b, j) for a, b in pairs for i in sides for j in sides]
     for partner in partners:
         pl.semaphore_signal(barrier, inc=1, device_id=partner, device_id_type=MESH)
 
     fetched[0].wait()
     tops = [jnp.abs(old[c, :, 0:128]) for c in range(3)]
-    for t in range(1, 2 * TILES):
+    for t in range(1, EACH * TILES):
         for c in range(3):
             tops[c] = jnp.maximum(tops[c], jnp.abs(old[c, :, 128 * t : 128 * t + 128]))
     top = jnp.maximum(jnp.maximum(tops[0], tops[1]), tops[2])
     meta[0, 0] = top * (1.0 / LEVELS)
     inverse = LEVELS / jnp.maximum(top, 1e-30)
     for kind in range(PARTS):
-        c, first = kind // 2, kind % 2 * TILES
+        c, first = kind // EACH, kind % EACH * TILES
         for t in range(TILES):
             begin = 128 * (first + t)
             staged[kind][pl.ds(t, SLOTS, stride=TILES), :] = jnp.round(old[c, :, begin : begin + 128] * inverse)
@@ -187,16 +186,24 @@
             keep_row(n, i, c, 0, layer, value[layer : layer + 1])
             keep_row(n, i, c, 1, layer, value[EDGE - 1 - layer : EDGE - layer])
 
-    def start_halo(n, tiles):
+    def start_faces(n, tiles):
         field = fields[n]
         for y in (1, 0):
-            send((n, "y", y), face_y[n][y], halo_y[n].at[1 - y], along("span", span, sides[y]))
+            send(
+                (n, "y", y),
+                face_y[n][y].at[pl.ds(0, 3)],
+                halo_y[n].at[1 - y, pl.ds(0, 3)],
+                along("span", span, sides[y]),
+            )
         for c in range(3):
             face_z[n][c] = pack_ends(tiles[c])
         for z in (0, 1):
             send((n, "z", z), face_z[n], halo_z[n].at[1 - z], along("depth", depth, sides[z]))
-        send((n, "x", 1), field.at[pl.ds(48, 6)], field.at[pl.ds(0, 6)], along("stream", stream, 1))
-        send((n, "x", 0), field.at[pl.ds(6, 6)], field.at[pl.ds(54, 6)], along("stream", stream, -1))
+        send((n, "x", 1), field.at[pl.ds(51, 3)], field.at[pl.ds(3, 3)], along("stream", stream, 1))
+        send((n, "x", 0), field.at[pl.ds(6, 3)], field.at[pl.ds(54, 3)], along("stream", stream, -1))
+
+    def start_diagonals(n):
+        field = fields[n]
         for x in (0, 1):
             for y in (0, 1):
                 send(
@@ -214,6 +221,15 @@
                         edge_z[n].at[4 * number + 3 - 2 * i - z],
                         diagonal(axis, sides[i], "depth", sides[z]),
                     )
+        for y in (1, 0):
+            send(
+                (n, "y2", y),
+                face_y[n][y].at[pl.ds(3, 3)],
+                halo_y[n].at[1 - y, pl.ds(3, 3)],
+                along("span", span, sides[y]),
+            )
+        send((n, "x2", 1), field.at[pl.ds(48, 3)], field.at[pl.ds(0, 3)], along("stream", stream, 1))
+        send((n, "x2", 0), field.at[pl.ds(9, 3)], field.at[pl.ds(57, 3)], along("stream", stream, -1))
 
     def ends(before, after, c, layer=1):
         low = jnp.where(depth == 0, 0.0, pltpu.roll(before[c], layer, 1))
@@ -228,26 +244,28 @@
 
             @pl.when(stream == end)
             def _():
-                fields[n][54 * x : 54 * x + 6] = jnp.zeros((6, EDGE, 128), jnp.float32)
+                fields[n][3 + 51 * x : 6 + 51 * x] = jnp.zeros((3, EDGE, 128), jnp.float32)
 
             @pl.when(span == end)
             def _():
-                halo_y[n][x] = jnp.zeros((6, EDGE, 128), jnp.float32)
+                halo_y[n][x, 0:3] = jnp.zeros((3, EDGE, 128), jnp.float32)
 
         return [ends(halo_z[n].at[0], halo_z[n].at[1], c) for c in range(3)]
 
     def finish_diagonals(n):
-        for key in [key for key in copies if key[0] == n and key[1] in ("xy", "stream", "span")]:
+        for key in [key for key in copies if key[0] == n and key[1] not in ("x", "y", "z")]:
             copies[key].wait_recv()
         for end, x in ((0, 0), (RING - 1, 1)):
 
             @pl.when(stream == end)
             def _():
+                fields[n][57 * x : 57 * x + 3] = jnp.zeros((3, EDGE, 128), jnp.float32)
                 for y in (0, 1):
                     corners_in[n][2 * x + y] = jnp.zeros(small, jnp.float32)
 
             @pl.when(span == end)
             def _():
+                halo_y[n][x, 3:6] = jnp.zeros((3, EDGE, 128), jnp.float32)
                 for y in (0, 1):
                     corners_in[n][2 * y + x] = jnp.zeros(small, jnp.float32)
 
@@ -320,7 +338,7 @@
             fields[2][(i + 2) * 3 + c] = value
             keep_faces(2, i, c, value)
             tiles[c] += [value[0:8], value[8:16]]
-    start_halo(2, tiles)
+    start_faces(2, tiles)
 
     def forward(kind, hop):
         copies[("r", kind, hop)].wait_recv()
@@ -337,10 +355,12 @@
 
     for kind in kinds:
         forward(kind, 2)
+    beyond = finish_faces(2)
+    start_diagonals(2)
 
     for kind in kinds:
         forward(kind, 3)
-    for kind in (PARTS, 0, 1, 2):
+    for kind in (PARTS, *range(PARTS // 2)):
         forward(kind, 4)
     for hop in range(5):
         copies[("c", PARTS, hop)].wait_recv()
@@ -383,8 +403,8 @@
 
     for kind in range(PARTS):
         pick(kind)
-        if kind + 3 < PARTS:
-            forward(kind + 3, 4)
+        for later in range(PARTS // 2, PARTS) if kind == 0 else ():
+            forward(later, 4)
 
     fetched[2].wait()
     group = lane // EDGE
@@ -401,7 +421,6 @@
         for c in range(3):
             pull[i * 3 + c] = level * share * forces[c]
 
-    beyond = finish_faces(2)
     halo = (beyond, *finish_diagonals(2))
     for k in range(3):
         carried_z[k] = ADVECT * halo[0][k]
@@ -422,7 +441,7 @@
         copies[("s", k)].wait_recv()
     tiles = [[], [], []]
     for kind in range(PARTS):
-        c, first = kind // 2, kind % 2 * (EDGE // 2)
+        c, first = kind // EACH, kind % EACH * (EDGE // EACH)
         for k in (2, 1, 3):
             copies[("x", kind, k)].wait_recv()
         for j in range(SLOTS):
@@ -439,8 +458,14 @@
                 at = 7 - layer if h else layer
                 keep_row(0, i, c, h, layer, tile[at : at + 1])
 
+    settled = set()
     for section in range(SECTIONS):
-        start_halo(section, tiles)
+        sent = [copy for key, copy in copies.items() if key not in settled]
+        settled.update(copies)
+        start_faces(section, tiles)
+        start_diagonals(section)
+        for copy in sent:
+            copy.wait_send()
         beyond = finish_faces(section)
         halo = (beyond, None, None)
         for i in (*range(EDGE), -1, EDGE):
@@ -483,15 +508,16 @@
                     keep_faces(section + 1, i, c, value)
                     tiles[c] += [value[0:8], value[8:16]]
 
-    for copy in copies.values():
-        copy.wait_send()
+    for key, copy in copies.items():
+        if key not in settled:
+            copy.wait_send()
 
 
 def body(old_adjoint, target, velocity, chi, fish, fish_forcing):
     f32, i16 = jnp.float32, jnp.int16
     v = pltpu.VMEM
     scratch = [
-        v((3, SLOTS, 2 * TILES * 128), f32),
+        v((3, SLOTS, EACH * TILES * 128), f32),
         v(velocity.shape, velocity.dtype),
         v(chi.shape, f32),
         [v((128, TILES, 128), i16)] * PARTS,

time: 63.4 us -> 62.4 us (0.984)
  Pallas kernels: 61.5 us -> 60.5 us
    pallas_call x1, Pallas kernels: 61.5 us -> 60.5 us  [body(): pl.pallas_call(kernel, out_shape=jax.ShapeDtypeStruct(velocity.shape, f32...]
where the time goes in v4:
time: 62.4 us; the launch traced here: 62.2 us
  Pallas kernels  60.5 us (97%)
  local copies, waits for them, and re-layouts  1.77 us (3%)
    pallas_call x1, Pallas kernels, body(): pl.pallas_call(kernel, out_shape=jax.ShapeDtypeStruct(velocity.shape, f32...  60.5 us
    unnamed x1, local copies, waits for them, and re-layouts  1.77 us

profile of v4, /device:TPU:1, one launch (start us, length us, event | category | flops | bytes accessed | tf_op | source)
XLA Modules:
  0.0 62.2 jit_solution(12885266595454829573)
XLA Ops:
  0.0 60.5 %shard_map.64 = f32[3,16,16,128]{3,2,1,0:T(8,128)} custom-call(s32[8]{0:T(128)} %target.1, s32[1,1,8]{2,1,0:T(1,128)} %fish.1, f32[3,64]{1,0:T(4,128)} %bitcast.1, f32[3,8,4096]{2,1,0:T(8,128)} %old_far.1, bf16[3,16,16,128]{3,2,1,0:T(8,128)(2,1)} %velocity_far.1, f32[16,16,128]{2,1,0:T(8,128)} %chi_far.1), custom_call_target="tpu_custom_call" | custom-call | tf_op jit(solution)/shard_map/pallas_call | solution.py:557
  60.5 1.8 %copy.8 = f32[3,16,16,128]{3,2,1,0:T(8,128)} copy(f32[3,16,16,128]{3,2,1,0:T(8,128)} %shard_map.64) | data formatting | bytes 786432

commit v5 on v4

--- a/solution.py
+++ b/solution.py
@@ -163,7 +163,7 @@
         count = 8 if hop in (0, 4) else 16
         send(("c", kind, hop), places(kind, first, count), places(kind, 8 + first, count), other_core)
 
-    kinds = (PARTS, *range(PARTS))
+    kinds = (0, PARTS, *range(1, PARTS))
     for kind in kinds:
         hop_right(kind, 1)
         hop_left(kind, 1)

time: 62.4 us -> 62.2 us (level)
  no operation moved by 1% of the time
where the time goes in v5:
time: 62.2 us; the launch traced here: 62.1 us
  Pallas kernels  60.3 us (97%)
  local copies, waits for them, and re-layouts  1.77 us (3%)
    pallas_call x1, Pallas kernels, body(): pl.pallas_call(kernel, out_shape=jax.ShapeDtypeStruct(velocity.shape, f32...  60.3 us
    unnamed x1, local copies, waits for them, and re-layouts  1.77 us

profile of v5, /device:TPU:1, one launch (start us, length us, event | category | flops | bytes accessed | tf_op | source)
XLA Modules:
  0.0 62.1 jit_solution(7219086592581222147)
XLA Ops:
  0.0 60.3 %shard_map.64 = f32[3,16,16,128]{3,2,1,0:T(8,128)} custom-call(s32[8]{0:T(128)} %target.1, s32[1,1,8]{2,1,0:T(1,128)} %fish.1, f32[3,64]{1,0:T(4,128)} %bitcast.1, f32[3,8,4096]{2,1,0:T(8,128)} %old_far.1, bf16[3,16,16,128]{3,2,1,0:T(8,128)(2,1)} %velocity_far.1, f32[16,16,128]{2,1,0:T(8,128)} %chi_far.1), custom_call_target="tpu_custom_call" | custom-call | tf_op jit(solution)/shard_map/pallas_call | solution.py:557
  60.3 1.8 %copy.8 = f32[3,16,16,128]{3,2,1,0:T(8,128)} copy(f32[3,16,16,128]{3,2,1,0:T(8,128)} %shard_map.64) | data formatting | bytes 786432
